TPU v7x, 512 devices: a whole 4x4x16 slice. The times are simulated.
512 devices in a mesh: row: 16 (over z_lo, y), col: 32 (over z_hi, x, core).
Axes of the slice: x: 4, y: 4, z: 16 (z_hi: 4, z_lo: 4; z = z_hi * 4 + z_lo), core: 2. Of those that a mesh axis runs over, the one named last changes fastest.
Arguments:
- tokens: bfloat16 [320, 12288], P('col', 'row'), may hold values from -6 to 6
- weight_in: bfloat16 [12288, 24576], P('row', 'col'), may hold values from -0.109375 to 0.109375
- weight_out: bfloat16 [24576, 12288], P('col', 'row'), may hold values from -0.078125 to 0.078125
- mask_in: int32 [96, 192], P('row', 'col'), may hold values 0 or 1
- mask_out: int32 [192, 96], P('col', 'row'), may hold values 0 or 1
- grad_out: bfloat16 [320, 12288], P('col', 'row'), may hold values from -6 to 6
Outputs:
- output: bfloat16 [320, 12288], P('col', 'row')
- grad_tokens: bfloat16 [320, 12288], P('col', 'row')
All inputs are finite; a program needn't handle non-finite values. No bound on the sum of `mask_in` or of `mask_out` on one device may be relied on, other than what follows from the above.
Results may differ from a plain program's by a relative error of at most 0.0049.
Values may be sent and summed in bfloat16 or wider, within the bound.
A program may use at most 64 MiB of HBM per device.

v0:
```python
import jax
import jax.numpy as jnp
from jax import lax
from jax.sharding import PartitionSpec as P


def expand(mask, rows):
    block = rows // mask.shape[0]
    blocks = mask.astype(jnp.bfloat16)
    return jnp.repeat(jnp.repeat(blocks, block, axis=0), block, axis=1)


def product_rows(left, right):
    return jnp.dot(left, right, preferred_element_type=jnp.float32)


def product_rows_trans(left, right):
    return lax.dot_general(
        left, right, (((1,), (1,)), ((), ())), preferred_element_type=jnp.float32
    )


def on_device(tokens, weight_in, weight_out, mask_in, mask_out, grad_out):
    keep_in = expand(mask_in, weight_in.shape[0])
    keep_out = expand(mask_out, weight_out.shape[0])
    masked_in = weight_in * keep_in
    masked_out = weight_out * keep_out
    all_tokens = lax.all_gather(tokens, "col", axis=0, tiled=True)
    pre_part = lax.psum_scatter(
        product_rows(all_tokens, masked_in), "row", scatter_dimension=0, tiled=True
    )
    hidden_part = jax.nn.gelu(pre_part).astype(jnp.bfloat16)
    hidden = lax.all_gather(hidden_part, "row", axis=0, tiled=True)
    output = lax.psum_scatter(
        product_rows(hidden, masked_out), "col", scatter_dimension=0, tiled=True
    )
    output = output.astype(jnp.bfloat16)
    all_grads = lax.all_gather(grad_out, "col", axis=0, tiled=True)
    grad_part = lax.psum_scatter(
        product_rows_trans(all_grads, masked_out), "row", scatter_dimension=0, tiled=True
    )
    _, pull = jax.vjp(jax.nn.gelu, pre_part)
    grad_pre_part = pull(grad_part)[0].astype(jnp.bfloat16)
    grad_pre = lax.all_gather(grad_pre_part, "row", axis=0, tiled=True)
    grad_tokens = lax.psum_scatter(
        product_rows_trans(grad_pre, masked_in), "col", scatter_dimension=0, tiled=True
    )
    grad_tokens = grad_tokens.astype(jnp.bfloat16)
    return (output, grad_tokens)


def solution(mesh):
    placed = (
        P("col", "row"),
        P("row", "col"),
        P("col", "row"),
        P("row", "col"),
        P("col", "row"),
        P("col", "row"),
    )
    return jax.shard_map(
        on_device,
        mesh=mesh,
        in_specs=placed,
        out_specs=(P("col", "row"), P("col", "row")),
        check_vma=False,
    )
```

profile of v0, /device:TPU:1, one launch (start us, length us, event | category | flops | bytes accessed | tf_op | source)
XLA Modules:
  0.0 474.2 jit_solution(10808497367819531498)
XLA Ops:
  0.6 0.0 copy-start.6
  0.6 0.0 copy-start.4
  0.7 1.6 copy.15
  2.2 0.0 copy-done.6
  2.3 0.1 copy.14
  2.4 0.1 broadcast_bitcast_fusion
  2.5 0.0 copy-done.4
  2.5 63.4 %all-gather.2 = bf16[32,10,768]{2,1,0:T(8,128)(2,1)S(1)} all-gather(bf16[1,10,768]{2,1,0:T(8,128)(2,1)S(1)} %bitcast.45), channel_id=1, replica_groups=mesh['row'=16,'col'=32] {'col'}, dimensions={0}, use_global_device_ids=true | all-gather | bytes 506880 | tf_op jit(solution)/shard_map/all_gather | solution.py:38
  65.9 1.0 reshape.25
  66.9 1.6 copy.13
  68.5 0.0 copy-done.7
  68.5 0.1 copy.12
  68.6 0.1 broadcast_bitcast_fusion.1
  68.7 0.6 copy.21
  69.3 50.0 %all-gather = bf16[32,10,768]{2,1,0:T(8,128)(2,1)S(1)} all-gather(bf16[1,10,768]{2,1,0:T(8,128)(2,1)S(1)} %bitcast.46), channel_id=1, replica_groups=mesh['row'=16,'col'=32] {'col'}, dimensions={0}, use_global_device_ids=true | all-gather | bytes 506880 | tf_op jit(solution)/shard_map/all_gather | solution.py:28
  119.3 1.0 reshape.21
  120.3 0.1 bitcast_multiply_fusion
  120.4 0.9 copy-done.1
  121.3 1.5 convolution_bitcast_fusion
  122.8 0.1 bitcast_multiply_fusion.1
  122.9 0.9 copy-done.2
  123.8 1.6 convolution_bitcast_fusion.1
  125.4 46.6 %fusion.11 = (f32[24,768]{1,0:T(8,128)S(1)}, f32[24,768]{1,0:T(8,128)S(1)}) fusion(f32[320,768]{1,0:T(8,128)} %convolution_bitcast_fusion.1, f32[320,768]{1,0:T(8,128)S(1)} %copy-done), kind=kCustom, calls=%all-reduce-scatter.2 | all-reduce-scatter fusion | flops 589825 | bytes 2115584
  172.0 1.3 collective-permute-start.3
  173.3 1.3 collective-permute-start.4
  174.6 1.3 collective-permute-start.5
  175.9 1.3 collective-permute-start
  177.2 1.9 collective-permute-start.1
  179.2 0.0 collective-permute-done.5
  179.2 4.8 %collective-permute-start.2 = (f32[12,768]{1,0:T(8,128)S(1)}, f32[12,768]{1,0:T(8,128)S(1)}, u32[]{:S(2)}, u32[]{:S(2)}) collective-permute-start(f32[12,768]{1,0:T(8,128)S(1)} %slice), channel_id=1, source_target_pairs={{0,96},{32,128},{64,160},{96,192},{128,224},{160,256},{192,288},{2... | collective-permute-start | bytes 110600
  184.0 1.3 dynamic-slice.10
  186.0 1.3 dynamic-slice.2
  187.9 0.0 collective-permute-done.3
  187.9 0.0 collective-permute-done.4
  187.9 0.5 concatenate.1
  188.4 0.0 collective-permute-done.2
  188.4 0.0 collective-permute-done
  188.4 0.0 collective-permute-done.1
  188.4 0.5 concatenate
  188.9 0.1 fusion.10
  189.0 33.1 %all-gather.3 = bf16[16,20,768]{2,1,0:T(8,128)(2,1)S(1)} all-gather(bf16[1,20,768]{2,1,0:T(8,128)(2,1)S(1)} %get-tuple-element.8), channel_id=1, replica_groups=mesh['row'=16,'col'=32] {'row'}, dimensions={0}, use_global_device_ids=true | all-gather | bytes 522240 | tf_op jit(solution)/shard_map/all_gather | solution.py:44
  222.0 0.9 reshape.27
  222.9 1.6 fusion.13
  224.5 35.0 %all-gather.1 = bf16[16,20,768]{2,1,0:T(8,128)(2,1)S(1)} all-gather(bf16[1,20,768]{2,1,0:T(8,128)(2,1)S(1)} %get-tuple-element.9), channel_id=1, replica_groups=mesh['row'=16,'col'=32] {'row'}, dimensions={0}, use_global_device_ids=true | all-gather | bytes 522240 | tf_op jit(solution)/shard_map/all_gather | solution.py:33
  259.5 0.9 reshape.23
  260.4 1.6 fusion.12
  262.0 211.6 %all-reduce.9 = (bf16[320,768]{1,0:T(8,128)(2,1)S(1)}, bf16[320,768]{1,0:T(8,128)(2,1)S(1)}) all-reduce(f32[320,768]{1,0:T(8,128)S(1)} %fusion.12, f32[320,768]{1,0:T(8,128)S(1)} %fusion.13), channel_id=3, replica_groups=mesh['row'=16,'col'=32] {'col'}, use_global_device_ids=true, to_apply=%region_1.0.clone | all-reduce | flops 491520 | bytes 2949120
  473.6 0.6 dynamic-slice_convert_fusion
  (14 shorter events, 0.0 us)
Async XLA Ops:
  0.6 1.6 copy-start.6
  0.6 1.8 copy-start.4
  66.9 1.6 copy-start.7
  66.9 2.4 copy-start.5
  120.3 1.0 copy-start.1
  121.3 1.5 copy-start.3
  122.8 1.0 copy-start.2
  123.8 1.6 copy-start
  172.0 15.9 %collective-permute-start.3 = (f32[24,768]{1,0:T(8,128)S(1)}, f32[24,768]{1,0:T(8,128)S(1)}, u32[]{:S(2)}, u32[]{:S(2)}) collective-permute-start(f32[24,768]{1,0:T(8,128)S(1)} %get-tuple-element.7), channel_id=1, source_target_pairs={{0,32},{32,64},{64,96},{96,128},{128,160},{160,192},{192,224},{224... | collective-permute-start | bytes 221192
  173.3 14.6 %collective-permute-start.4 = (f32[24,768]{1,0:T(8,128)S(1)}, f32[24,768]{1,0:T(8,128)S(1)}, u32[]{:S(2)}, u32[]{:S(2)}) collective-permute-start(f32[24,768]{1,0:T(8,128)S(1)} %get-tuple-element.7), channel_id=1, source_target_pairs={{0,64},{32,96},{64,128},{96,160},{128,192},{160,224},{192,256},{22... | collective-permute-start | bytes 221192
  174.6 4.6 collective-permute-start.5
  175.9 12.5 %collective-permute-start = (f32[24,768]{1,0:T(8,128)S(1)}, f32[24,768]{1,0:T(8,128)S(1)}, u32[]{:S(2)}, u32[]{:S(2)}) collective-permute-start(f32[24,768]{1,0:T(8,128)S(1)} %get-tuple-element.6), channel_id=1, source_target_pairs={{0,32},{32,64},{64,96},{96,128},{128,160},{160,192},{192,224},{224... | collective-permute-start | bytes 221192
  177.2 11.2 %collective-permute-start.1 = (f32[24,768]{1,0:T(8,128)S(1)}, f32[24,768]{1,0:T(8,128)S(1)}, u32[]{:S(2)}, u32[]{:S(2)}) collective-permute-start(f32[24,768]{1,0:T(8,128)S(1)} %get-tuple-element.6), channel_id=1, source_target_pairs={{0,64},{32,96},{64,128},{96,160},{128,192},{160,224},{192,256},{22... | collective-permute-start | bytes 221192
  179.2 9.2 %collective-permute-start.2 = (f32[12,768]{1,0:T(8,128)S(1)}, f32[12,768]{1,0:T(8,128)S(1)}, u32[]{:S(2)}, u32[]{:S(2)}) collective-permute-start(f32[12,768]{1,0:T(8,128)S(1)} %slice), channel_id=1, source_target_pairs={{0,96},{32,128},{64,160},{96,192},{128,224},{160,256},{192,288},{2... | collective-permute-start | bytes 110600
where the time goes:
time: 481 us; the launch traced here: 474 us
  blocking collectives  440 us (91%)
  local copies, waits for them, and re-layouts  13.9 us (3%)
  starting transfers between devices  11.9 us (2%)
  matrix products  6.26 us (1%)
    unnamed x2, blocking collectives  258 us
    all_gather x1, blocking collectives, on_device(): all_grads = lax.all_gather(grad_out, 'col', axis=0, tiled=True)  63.4 us
    all_gather x1, blocking collectives, on_device(): all_tokens = lax.all_gather(tokens, 'col', axis=0, tiled=True)  50 us
    all_gather x1, blocking collectives, on_device(): hidden = lax.all_gather(hidden_part, 'row', axis=0, tiled=True)  35 us
    all_gather x1, blocking collectives, on_device(): grad_pre = lax.all_gather(grad_pre_part, 'row', axis=0, tiled=True)  33.1 us
    unnamed x32, local copies, waits for them, and re-layouts  13 us
    unnamed x6, starting transfers between devices  11.9 us
  transfers between devices with their start and end apart: 6, of which 0 were waited for; matrix products, arithmetic and copies ran while one was open for 1% of the time, Pallas kernels for 0%

commit v1 on v0

v1 whole, which is shorter than its diff:
```python
import jax
import jax.numpy as jnp
from jax import lax
from jax.experimental import pallas as pl
from jax.experimental.pallas import tpu as pltpu
from jax.sharding import PartitionSpec as P

F32, BF16 = jnp.float32, jnp.bfloat16
MESH = pl.DeviceIdType.MESH
PARTS = 2
M = 6 // PARTS
WIDE = 128 * M
ROWS = 80 * M
SHARE = -(-(20 * M) // 16) * 16
N_SEMS = 20 + 2 * PARTS * 21 + 20


def nn(a, b):
    return jnp.dot(a, b, preferred_element_type=F32)


def nt(a, b):
    return lax.dot_general(a, b, (((1,), (1,)), ((), ())), preferred_element_type=F32)


def lanes_to_rows(v):
    return jnp.concatenate(
        [v[:, 128 * j : 128 * (j + 1)] for j in range(v.shape[1] // 128)], axis=0
    )


def sigmoid_parts(v):
    u = 0.7978845608028654 * (v + 0.044715 * (v * v * v))
    return 1.0 / (1.0 + jnp.exp(jnp.minimum(-2.0 * u, 80.0)))


def kernel(
    mask_in, mask_out, tok, grad, w_in_hbm, w_out_hbm, out, gtok,
    w_in, w_out, gath, pack, unp, lhs, part_f, part_b, y_in, half_f, half_b, z_in, pre_s,
    hid, acc, sib_out, sib_in, x_out, x_in, mine, piece, zh_out, zh_in,
    w_sem, send, recv,
):
    r, c = lax.axis_index("row"), lax.axis_index("col")
    zl, y = r // 4, r % 4
    zh, x, k = c // 8, (c // 2) % 4, c % 2

    def at_y(d):
        return {"row": zl * 4 + (y + d) % 4}

    def at_zl(d):
        return {"row": ((zl + d) % 4) * 4 + y}

    def at_x(d):
        return {"col": zh * 8 + ((x + d) % 4) * 2 + k}

    def at_zh(d):
        return {"col": ((zh + d) % 4) * 8 + x * 2 + k}

    sibling = {"col": zh * 8 + x * 2 + (1 - k)}

    loads = [
        pltpu.make_async_copy(w_in_hbm, w_in, w_sem.at[0]),
        pltpu.make_async_copy(w_out_hbm, w_out, w_sem.at[1]),
    ]
    for load in loads:
        load.start()

    barrier = pltpu.get_barrier_semaphore()
    peers = [sibling]
    for d in (1, 2, 3):
        peers += [at_zh(d), at_x(d), at_y(d), at_zl(d)]
    for peer in peers:
        pl.semaphore_signal(barrier, inc=1, device_id=peer, device_id_type=MESH)

    started = []

    def put(src, dst, peer):
        i = len(started)
        copy = pltpu.make_async_remote_copy(
            src_ref=src, dst_ref=dst, send_sem=send.at[i], recv_sem=recv.at[i],
            device_id=peer, device_id_type=MESH,
        )
        copy.start()
        started.append(copy)
        return copy

    ins, outs = (tok, grad), (out, gtok)
    for a in (0, 1):
        v = ins[a][...].astype(F32)
        pack[a] = jnp.zeros((64, 128), F32)
        for j in range(6):
            pack[a, pl.ds(j, 10, stride=6), :] = v[:, 128 * j : 128 * (j + 1)]
        gath[a, 0, 0, 0] = pack[a].astype(BF16)
        for e in range(4):
            piece[a, e, pl.ds(56, 8), :] = jnp.zeros((8, 128), F32)
    pl.semaphore_wait(barrier, len(peers))

    zs = [
        [put(gath.at[a, 0, 0, 0], gath.at[a, 0, 0, 4 - d], at_zh(d)) for d in (1, 2, 3)]
        for a in (0, 1)
    ]
    for load in loads:
        load.wait()
    for w, mask in ((w_in, mask_in), (w_out, mask_out)):
        for i in range(6):
            rows = slice(128 * i, 128 * (i + 1))
            for j in range(6):
                cols = slice(128 * j, 128 * (j + 1))
                keep = mask[i, j].astype(F32)
                w[rows, cols] = (w[rows, cols].astype(F32) * keep).astype(BF16)
    xs, sibs = [], []
    for a in (0, 1):
        for copy in zs[a]:
            copy.wait_recv()
        xs.append(
            [put(gath.at[a, 0, 0], gath.at[a, 4 - d, 0], at_x(d)) for d in (1, 2, 3)]
        )
        sibs.append([put(gath.at[a, 0, 0], gath.at[a, 0, 1], sibling)])
    ys = {}
    for a in (0, 1):
        for d in (1, 2, 3):
            xs[a][d - 1].wait_recv()
            sibs[a].append(put(gath.at[a, 4 - d, 0], gath.at[a, 4 - d, 1], sibling))
        for copy in sibs[a]:
            copy.wait_recv()
        for s in range(32):
            d, dk, e = s // 8, (s // 4) % 2, s % 4
            unp[pl.ds(60 * s, 60), :] = gath[a, d, dk, e].astype(F32)[:60]
        for j in range(6):
            lhs[:, 128 * j : 128 * (j + 1)] = unp[pl.ds(j, 320, stride=6), :].astype(BF16)
        for n in range(PARTS):
            cols = slice(WIDE * n, WIDE * (n + 1))
            if a == 0:
                value = nn(lhs[...], w_in[:, cols])
            else:
                value = nt(lhs[...], w_out[cols, :])
            for g in range(4):
                rows = lanes_to_rows(value[80 * g : 80 * (g + 1)])
                part_f[a, n, g] = rows
                part_b[a, n, g] = rows.astype(BF16)
            ys[a, n] = [
                put(part_b.at[a, n, (y + d) % 4], y_in.at[a, n, 4 - d], at_y(d))
                for d in (1, 2, 3)
            ]

    units = [(a, n) for a in (0, 1) for n in range(PARTS)]
    zls, own = {}, {}
    for a, n in units:
        for copy in ys[a, n]:
            copy.wait_recv()
        total = part_f[a, n, y]
        for d in (1, 2, 3):
            total = total + y_in[a, n, d].astype(F32)
        if 4 * SHARE > ROWS:
            total = jnp.concatenate([total, jnp.zeros((4 * SHARE - ROWS, 128), F32)], axis=0)
        for q in range(4):
            rows = total[SHARE * q : SHARE * (q + 1)]
            half_f[a, n, q] = rows
            half_b[a, n, q] = rows.astype(BF16)
        zls[a, n] = [
            put(half_b.at[a, n, (zl + d) % 4], z_in.at[a, n, 4 - d], at_zl(d))
            for d in (1, 2, 3)
        ]
    gz, gy = {}, {}
    for a, n in units:
        for copy in zls[a, n]:
            copy.wait_recv()
        total = half_f[a, n, zl]
        for d in (1, 2, 3):
            total = total + z_in[a, n, d].astype(F32)
        if a == 0:
            pre_s[n] = total
            value = total * sigmoid_parts(total)
        else:
            v = pre_s[n]
            s = sigmoid_parts(v)
            slope = 1.5957691216057308 * (1.0 + 0.134145 * (v * v))
            value = (s + v * (s * (1.0 - s)) * slope) * total
        hid[a, n, y, zl] = value.astype(BF16)
        slot = hid.at[a, n, y, zl]
        gz[a, n] = [put(slot, slot, at_zl(d)) for d in (1, 2, 3)]
        gy[a, n] = [put(slot, slot, at_y(d)) for d in (1, 2, 3)]
    for a, n in units:
        for d in (1, 2, 3):
            gz[a, n][d - 1].wait_recv()
            slot = hid.at[a, n, y, (zl + 4 - d) % 4]
            gy[a, n] += [put(slot, slot, at_y(e)) for e in (1, 2, 3)]
    pairs = []
    for a in (0, 1):
        for n in range(PARTS):
            for copy in gy[a, n]:
                copy.wait_recv()
            cols = slice(WIDE * n, WIDE * (n + 1))
            left = jnp.concatenate(
                [
                    jnp.concatenate(
                        [
                            hid[a, n, g].reshape(4 * SHARE, 128)[80 * j : 80 * (j + 1)]
                            for j in range(M)
                        ],
                        axis=1,
                    )
                    for g in range(4)
                ],
                axis=0,
            )
            if a == 0:
                value = nn(left, w_out[cols, :])
            else:
                value = nt(left, w_in[:, cols])
            if n:
                value = value + acc[...]
            if n + 1 < PARTS:
                acc[...] = value
        pair = []
        for d in range(4):
            mine[a, d] = lanes_to_rows(value[80 * d : 80 * d + 40])
            sib_out[a, d] = lanes_to_rows(value[80 * d + 40 : 80 * d + 80])
        for d in (1, 2, 3, 0):
            pair.append(put(sib_out.at[a, d], sib_in.at[a, d], sibling))
        pairs.append(pair)
    xr = []
    for a in (0, 1):
        got = []
        for i, d in enumerate((1, 2, 3, 0)):
            pairs[a][i].wait_recv()
            total = mine[a, d] + sib_in[a, d]
            if d:
                x_out[a, d] = total.astype(BF16)
                got.append(put(x_out.at[a, d], x_in.at[a, 4 - d], at_x(d)))
            else:
                mine[a, 0] = total
        xr.append(got)
    zr = []
    for a in (0, 1):
        for copy in xr[a]:
            copy.wait_recv()
        total = mine[a, 0]
        for d in (1, 2, 3):
            total = total + x_in[a, d].astype(F32)
        mine[a, 0] = total
        for e in (1, 2, 3, 0):
            for j in range(6):
                piece[a, e, pl.ds(10 * j, 10), :] = mine[a, 0, pl.ds(40 * j + 10 * e, 10), :]
            if e:
                zh_out[a, e] = piece[a, e].astype(BF16)
        zr.append(
            [put(zh_out.at[a, e], zh_in.at[a, 4 - e], at_zh(e)) for e in (1, 2, 3)]
        )
    for a in (0, 1):
        for copy in zr[a]:
            copy.wait_recv()
        total = piece[a, 0]
        for e in (1, 2, 3):
            total = total + zh_in[a, e].astype(F32)
        piece[a, 0] = total
        outs[a][...] = jnp.concatenate(
            [piece[a, 0, pl.ds(10 * j, 10), :] for j in range(6)], axis=1
        ).astype(BF16)
    for copy in started:
        copy.wait_send()


def on_device(tokens, weight_in, weight_out, mask_in, mask_out, grad_out):
    vmem = pl.BlockSpec(memory_space=pltpu.VMEM)
    smem = pl.BlockSpec(memory_space=pltpu.SMEM)
    hbm = pl.BlockSpec(memory_space=pl.ANY)
    shape = jax.ShapeDtypeStruct(tokens.shape, BF16)
    return pl.pallas_call(
        kernel,
        out_shape=(shape, shape),
        in_specs=[smem, smem, vmem, vmem, hbm, hbm],
        out_specs=(vmem, vmem),
        scratch_shapes=[
            pltpu.VMEM((768, 768), BF16),
            pltpu.VMEM((768, 768), BF16),
            pltpu.VMEM((2, 4, 2, 4, 64, 128), BF16),
            pltpu.VMEM((2, 64, 128), F32),
            pltpu.VMEM((1920, 128), F32),
            pltpu.VMEM((320, 768), BF16),
            pltpu.VMEM((2, PARTS, 4, ROWS, 128), F32),
            pltpu.VMEM((2, PARTS, 4, ROWS, 128), BF16),
            pltpu.VMEM((2, PARTS, 4, ROWS, 128), BF16),
            pltpu.VMEM((2, PARTS, 4, SHARE, 128), F32),
            pltpu.VMEM((2, PARTS, 4, SHARE, 128), BF16),
            pltpu.VMEM((2, PARTS, 4, SHARE, 128), BF16),
            pltpu.VMEM((PARTS, SHARE, 128), F32),
            pltpu.VMEM((2, PARTS, 4, 4, SHARE, 128), BF16),
            pltpu.VMEM((320, 768), F32),
            pltpu.VMEM((2, 4, 240, 128), F32),
            pltpu.VMEM((2, 4, 240, 128), F32),
            pltpu.VMEM((2, 4, 240, 128), BF16),
            pltpu.VMEM((2, 4, 240, 128), BF16),
            pltpu.VMEM((2, 4, 240, 128), F32),
            pltpu.VMEM((2, 4, 64, 128), F32),
            pltpu.VMEM((2, 4, 64, 128), BF16),
            pltpu.VMEM((2, 4, 64, 128), BF16),
            pltpu.SemaphoreType.DMA((2,)),
            pltpu.SemaphoreType.DMA((N_SEMS,)),
            pltpu.SemaphoreType.DMA((N_SEMS,)),
        ],
        compiler_params=pltpu.CompilerParams(
            collective_id=0, has_side_effects=True, vmem_limit_bytes=48 * 2**20
        ),
    )(mask_in, mask_out, tokens, grad_out, weight_in, weight_out)


def solution(mesh):
    placed = (
        P("col", "row"),
        P("row", "col"),
        P("col", "row"),
        P("row", "col"),
        P("col", "row"),
        P("col", "row"),
    )
    return jax.shard_map(
        on_device,
        mesh=mesh,
        in_specs=placed,
        out_specs=(P("col", "row"), P("col", "row")),
        check_vma=False,
    )
```

time: 481 us -> 88 us (0.18); the launches traced: 474 us -> 87.6 us
  blocking collectives: 440 us -> 0 us
  Pallas kernels: 0 us -> 80.3 us
  starting transfers between devices: 11.9 us -> 0 us
  local copies, waits for them, and re-layouts: 13.9 us -> 6.6 us
  matrix products: 6.26 us -> 0 us
    unnamed x2 -> x0, blocking collectives: 258 us -> none
    all_gather x4 -> x0, blocking collectives: 182 us -> none  [the longest x1 63.4 us: on_device(): all_grads = lax.all_gather(grad_out, 'col', axis=0, tiled=True)]
    pallas_call x0 -> x1, Pallas kernels: none -> 80.3 us  [on_device(): pl.pallas_call(kernel, out_shape=(shape, shape), in_specs=[smem, smem, vm...]
    unnamed x6 -> x0, starting transfers between devices: 11.9 us -> none
    unnamed x32 -> x14, local copies, waits for them, and re-layouts: 13 us -> 6.6 us
    dot_general x4 -> x0, matrix products: 6.26 us -> none  [the longest x2 3.18 us: product_rows(): return jnp.dot(left, right, preferred_element_type=jnp.float32)]
  transfers between devices with their start and end apart: 6 -> 0, of which waited for: 0 -> 0; matrix products, arithmetic and copies ran while one was open for 1% -> 0% of each run, Pallas kernels for 0% -> 0%
where the time goes in v1:
time: 88 us; the launch traced here: 87.6 us
  Pallas kernels  80.3 us (91%)
  local copies, waits for them, and re-layouts  6.6 us (8%)
    pallas_call x1, Pallas kernels, on_device(): pl.pallas_call(kernel, out_shape=(shape, shape), in_specs=[smem, smem, vm...  80.3 us
    unnamed x14, local copies, waits for them, and re-layouts  6.6 us

profile of v1, /device:TPU:1, one launch (start us, length us, event | category | flops | bytes accessed | tf_op | source)
XLA Modules:
  0.0 87.6 jit_solution(10736415613996347030)
XLA Ops:
  0.6 0.0 copy-start
  0.6 1.3 %copy-done = bf16[768,768]{1,0:T(8,128)(2,1)S(1)} copy-done((bf16[768,768]{1,0:T(8,128)(2,1)S(1)}, bf16[768,768]{1,0:T(8,128)(2,1)}, u32[]{:S(2)}) %copy-start) | copy-done | bytes 1179672
  1.9 0.0 copy-start.1
  1.9 1.3 %copy-done.1 = bf16[768,768]{1,0:T(8,128)(2,1)S(1)} copy-done((bf16[768,768]{1,0:T(8,128)(2,1)S(1)}, bf16[768,768]{1,0:T(8,128)(2,1)}, u32[]{:S(2)}) %copy-start.1) | copy-done | bytes 1179672
  3.2 0.0 copy-start.2
  3.2 0.7 copy-done.2
  3.9 0.0 copy-start.3
  3.9 0.7 copy-done.3
  4.7 0.0 copy-start.4
  4.7 0.7 copy-done.4
  5.3 0.0 copy-start.5
  5.3 0.7 copy-done.5
  6.0 80.3 %shard_map.77 = (bf16[10,768]{1,0:T(8,128)(2,1)S(1)}, bf16[10,768]{1,0:T(8,128)(2,1)S(1)}) custom-call(s32[6,6]{1,0:T(8,128)S(1)} %copy-done.4, s32[6,6]{1,0:T(8,128)S(1)} %copy-done.5, bf16[10,768]{1,0:T(8,128)(2,1)S(1)} %copy-done.2, bf16[10,768]{1,0:T(8,128)(2,1)S(1)} %copy-done.3, bf16[768,768]{1,0:T(8,128)(2,1)S(1)} %copy-done, ...), custom_call_target="tpu_custom_call" | custom-call | tf_op jit(solution)/shard_map/pallas_call | solution.py:269
  86.4 0.6 copy.10
  87.0 0.6 copy.11
Async XLA Ops:
  0.6 1.3 %copy-start = (bf16[768,768]{1,0:T(8,128)(2,1)S(1)}, bf16[768,768]{1,0:T(8,128)(2,1)}, u32[]{:S(2)}) copy-start(bf16[768,768]{1,0:T(8,128)(2,1)} %w_in_hbm.1) | copy-start | bytes 3538948
  1.9 1.3 %copy-start.1 = (bf16[768,768]{1,0:T(8,128)(2,1)S(1)}, bf16[768,768]{1,0:T(8,128)(2,1)}, u32[]{:S(2)}) copy-start(bf16[768,768]{1,0:T(8,128)(2,1)} %w_out_hbm.1) | copy-start | bytes 3538948
  3.2 0.7 copy-start.2
  3.9 0.7 copy-start.3
  4.7 0.7 copy-start.4
  5.3 0.7 copy-start.5

commit v2 on v0

v2 whole, which is shorter than its diff:
```python
import jax
import jax.numpy as jnp
from jax import lax
from jax.experimental import pallas as pl
from jax.experimental.pallas import tpu as pltpu
from jax.sharding import PartitionSpec as P

F32, BF16 = jnp.float32, jnp.bfloat16
MESH = pl.DeviceIdType.MESH
PLACES = (0, 1, 3, 2)
ORDER = (
    (1, 0, 0), (1, 1, 0), (0, 0, 1), (0, 0, 2), (0, 0, 3), (1, 0, 1), (0, 1, 1), (1, 0, 2),
    (0, 1, 2), (1, 0, 3), (0, 1, 3), (1, 1, 1), (2, 0, 0), (1, 1, 2), (1, 1, 3), (2, 1, 0),
    (2, 0, 1), (3, 0, 0), (2, 0, 2), (3, 1, 0), (2, 0, 3), (2, 1, 1), (3, 0, 1), (2, 1, 2),
    (4, 0, 0), (3, 0, 2), (2, 1, 3), (4, 1, 0), (3, 0, 3), (3, 1, 1), (4, 0, 1), (3, 1, 2),
    (5, 0, 0), (4, 0, 2), (3, 1, 3), (5, 1, 0), (6, 0, 0), (4, 0, 3), (4, 1, 1), (6, 1, 0),
    (5, 0, 1), (4, 1, 2), (5, 0, 2), (6, 0, 1), (4, 1, 3), (5, 0, 3), (6, 0, 2), (5, 1, 1),
    (6, 0, 3), (5, 1, 2), (6, 1, 1), (5, 1, 3), (6, 1, 2), (6, 1, 3), (7, 0, 0), (7, 1, 0),
)
N_SEMS = 34 + 8 * 21 + 20


def nn(a, b):
    return jnp.dot(a, b, preferred_element_type=F32)


def nt(a, b):
    return lax.dot_general(a, b, (((1,), (1,)), ((), ())), preferred_element_type=F32)


def lanes_to_rows(v):
    return jnp.concatenate(
        [v[:, 128 * j : 128 * (j + 1)] for j in range(v.shape[1] // 128)], axis=0
    )


def sigmoid_2u(v):
    u = 0.7978845608028654 * (v + 0.044715 * (v * v * v))
    return 1.0 / (1.0 + jnp.exp(jnp.minimum(-2.0 * u, 80.0)))


def kernel(
    mask_in_hbm, mask_out_hbm, tok_hbm, grad_hbm, w_in_hbm, w_out_hbm, out, gtok,
    mask_in, mask_out, tok, grad, w_in, w_out, gath, pack, unp, part_f, part_b, y_in,
    half_f, half_b, z_in, pre_s, hid, sib_out, sib_in, x_out, x_in, mine, piece, zh_out, zh_in,
    load_sem, send, recv,
):
    r, c = lax.axis_index("row"), lax.axis_index("col")
    zl, y = r // 4, r % 4
    zh, x, k = c // 8, (c // 2) % 4, c % 2

    def at_y(d):
        return {"row": zl * 4 + (y + d) % 4}

    def at_zl(d):
        return {"row": ((zl + d) % 4) * 4 + y}

    def at_x(d):
        return {"col": zh * 8 + ((x + d) % 4) * 2 + k}

    def at_zh(d):
        return {"col": ((zh + d) % 4) * 8 + x * 2 + k}

    sibling = {"col": zh * 8 + x * 2 + (1 - k)}

    barrier = pltpu.get_barrier_semaphore()
    peers = [at_zh(1), at_zh(3)]
    for d in (2, 1, 3):
        peers += [at_x(d), at_y(d), at_zl(d)]
    peers.append(sibling)
    for peer in peers:
        pl.semaphore_signal(barrier, inc=1, device_id=peer, device_id_type=MESH)

    loads = []
    for src, dst in (
        (tok_hbm, tok),
        (grad_hbm, grad),
        (mask_in_hbm, mask_in),
        (mask_out_hbm, mask_out),
        (w_in_hbm, w_in),
        (w_out_hbm, w_out),
    ):
        loads.append(pltpu.make_async_copy(src, dst, load_sem.at[len(loads)]))
        loads[-1].start()

    started = []

    def put(src, dst, peer):
        i = len(started)
        copy = pltpu.make_async_remote_copy(
            src_ref=src, dst_ref=dst, send_sem=send.at[i], recv_sem=recv.at[i],
            device_id=peer, device_id_type=MESH,
        )
        copy.start()
        started.append(copy)
        return copy

    def arrive(copies):
        for copy in copies:
            copy.wait_recv()

    for a, v in ((0, tok), (1, grad)):
        loads[a].wait()
        v = v[...].astype(F32)
        pack[a] = jnp.zeros((64, 128), F32)
        for j in range(6):
            pack[a, pl.ds(j, 10, stride=6), :] = v[:, 128 * j : 128 * (j + 1)]
        gath[a, 0, 0, 0] = pack[a].astype(BF16)
        for e in range(4):
            piece[a, e, pl.ds(56, 8), :] = jnp.zeros((8, 128), F32)
    pl.semaphore_wait(barrier, len(peers))

    near, far, xs, sibs = {}, {}, {}, {}

    def spread(a, lo, hi):
        src = gath.at[a, 0, 0, pl.ds(lo, hi - lo)]
        for d in (1, 3, 2):
            dst = gath.at[a, 4 - d, 0, pl.ds(lo, hi - lo)]
            xs.setdefault((a, 4 - d), []).append(put(src, dst, at_x(d)))

    for a in (0, 1):
        own = gath.at[a, 0, 0, 0]
        near[a] = [put(own, gath.at[a, 0, 0, 2], at_zh(1)), put(own, gath.at[a, 0, 0, 1], at_zh(3))]
    for a in (0, 1):
        spread(a, 0, 1)
    for load in loads[2:]:
        load.wait()
    for w, mask in ((w_in, mask_in), (w_out, mask_out)):
        for i in range(6):
            rows = slice(128 * i, 128 * (i + 1))
            for j in range(6):
                cols = slice(128 * j, 128 * (j + 1))
                keep = mask[i, j].astype(F32)
                w[rows, cols] = (w[rows, cols].astype(F32) * keep).astype(BF16)
    for a in (0, 1):
        arrive(near[a])
        top, low = pl.ds(0, 32), pl.ds(32, 32)
        far[a] = [
            put(gath.at[a, 0, 0, 1, top], gath.at[a, 0, 0, 3, top], at_zh(3)),
            put(gath.at[a, 0, 0, 2, low], gath.at[a, 0, 0, 3, low], at_zh(1)),
        ]
        spread(a, 1, 3)
    for a in (0, 1):
        arrive(far[a])
        sibs[a, 0] = put(gath.at[a, 0, 0], gath.at[a, 0, 1], sibling)
        spread(a, 3, 4)

    ys, zls, gz, gy, pairs, xr, zr = {}, {}, {}, {}, {}, {}, {}

    def to_sibling(a, d):
        arrive(xs[a, d])
        sibs[a, d] = put(gath.at[a, d, 0], gath.at[a, d, 1], sibling)

    def first_product(a, d):
        arrive([sibs[a, d]])
        for s in range(8):
            unp[a, pl.ds(60 * s, 60), :] = gath[a, d, s // 4, s % 4].astype(F32)[:60]
        left = jnp.concatenate(
            [unp[a, pl.ds(j, 80, stride=6), :].astype(BF16) for j in range(6)], axis=1
        )
        value = nn(left, w_in[...]) if a == 0 else nt(left, w_out[...])
        rows = jnp.concatenate([lanes_to_rows(value), jnp.zeros((32, 128), F32)], axis=0)
        for g in range(4):
            part = rows[128 * g : 128 * (g + 1)]
            part_f[a, d, g] = part
            part_b[a, d, g] = part.astype(BF16)
        ys[a, d] = [
            put(part_b.at[a, d, (y + e) % 4], y_in.at[a, d, 4 - e], at_y(e)) for e in (1, 3, 2)
        ]

    def sum_over_y(a, d):
        arrive(ys[a, d])
        total = part_f[a, d, y]
        for e in (1, 2, 3):
            total = total + y_in[a, d, e].astype(F32)
        for q in range(4):
            rows = total[32 * q : 32 * (q + 1)]
            half_f[a, d, q] = rows
            half_b[a, d, q] = rows.astype(BF16)
        zls[a, d] = [
            put(half_b.at[a, d, (zl + e) % 4], z_in.at[a, d, 4 - e], at_zl(e)) for e in (2, 1, 3)
        ]

    def activate(a, d):
        arrive(zls[a, d])
        total = half_f[a, d, zl]
        for e in (1, 2, 3):
            total = total + z_in[a, d, e].astype(F32)
        if a == 0:
            pre_s[d] = total
            value = total * sigmoid_2u(total)
        else:
            v = pre_s[d]
            s = sigmoid_2u(v)
            slope = 1.5957691216057308 * (1.0 + 0.134145 * (v * v))
            value = (s + v * (s * (1.0 - s)) * slope) * total
        hid[a, d, y, zl] = value.astype(BF16)
        slot = hid.at[a, d, y, zl]
        gz[a, d] = [put(slot, slot, at_zl(e)) for e in (1, 2, 3)]
        gy[a, d] = [put(slot, slot, at_y(e)) for e in (1, 3, 2)]

    def pass_on(a, d):
        for e in (1, 2, 3):
            arrive([gz[a, d][e - 1]])
            slot = hid.at[a, d, y, (zl + 4 - e) % 4]
            gy[a, d] += [put(slot, slot, at_y(f)) for f in (1, 3, 2)]

    def second_product(a, d):
        arrive(gy[a, d])
        rows = hid[a, d].reshape(512, 128)
        left = jnp.concatenate([rows[80 * j : 80 * (j + 1)] for j in range(6)], axis=1)
        value = nn(left, w_out[...]) if a == 0 else nt(left, w_in[...])
        mine[a, d] = lanes_to_rows(value[:40])
        sib_out[a, d] = lanes_to_rows(value[40:])
        pairs[a, d] = put(sib_out.at[a, d], sib_in.at[a, d], sibling)

    def sum_over_cores(a, d):
        arrive([pairs[a, d]])
        total = mine[a, d] + sib_in[a, d]
        if d:
            x_out[a, d] = total.astype(BF16)
            xr[a, d] = put(x_out.at[a, d], x_in.at[a, 4 - d], at_x(d))
        else:
            mine[a, 0] = total

    def sum_over_x(a, _):
        arrive([xr[a, d] for d in (1, 2, 3)])
        total = mine[a, 0]
        for d in (1, 2, 3):
            total = total + x_in[a, d].astype(F32)
        mine[a, 0] = total
        zr[a] = []
        for p in (3, 1, 2, 0):
            e = PLACES[p]
            for j in range(6):
                piece[a, p, pl.ds(10 * j, 10), :] = mine[a, 0, pl.ds(40 * j + 10 * p, 10), :]
            if e:
                zh_out[a, p] = piece[a, p].astype(BF16)
                zr[a].append(put(zh_out.at[a, p], zh_in.at[a, 4 - e], at_zh(e)))

    stages = (
        to_sibling, first_product, sum_over_y, activate, pass_on, second_product,
        sum_over_cores, sum_over_x,
    )
    for stage, a, d in ORDER:
        stages[stage](a, d)
    for a, ref in ((0, out), (1, gtok)):
        arrive(zr[a])
        total = piece[a, 0]
        for e in (1, 2, 3):
            total = total + zh_in[a, e].astype(F32)
        piece[a, 0] = total
        ref[...] = jnp.concatenate(
            [piece[a, 0, pl.ds(10 * j, 10), :] for j in range(6)], axis=1
        ).astype(BF16)
    for copy in started:
        copy.wait_send()


def on_device(tokens, weight_in, weight_out, mask_in, mask_out, grad_out):
    vmem = pl.BlockSpec(memory_space=pltpu.VMEM)
    hbm = pl.BlockSpec(memory_space=pltpu.HBM)
    shape = jax.ShapeDtypeStruct(tokens.shape, BF16)
    return pl.pallas_call(
        kernel,
        out_shape=(shape, shape),
        in_specs=[hbm] * 6,
        out_specs=(vmem, vmem),
        scratch_shapes=[
            pltpu.SMEM(mask_in.shape, jnp.int32),
            pltpu.SMEM(mask_out.shape, jnp.int32),
            pltpu.VMEM(tokens.shape, BF16),
            pltpu.VMEM(tokens.shape, BF16),
            pltpu.VMEM((768, 768), BF16),
            pltpu.VMEM((768, 768), BF16),
            pltpu.VMEM((2, 4, 2, 4, 64, 128), BF16),
            pltpu.VMEM((2, 64, 128), F32),
            pltpu.VMEM((2, 480, 128), F32),
            pltpu.VMEM((2, 4, 4, 128, 128), F32),
            pltpu.VMEM((2, 4, 4, 128, 128), BF16),
            pltpu.VMEM((2, 4, 4, 128, 128), BF16),
            pltpu.VMEM((2, 4, 4, 32, 128), F32),
            pltpu.VMEM((2, 4, 4, 32, 128), BF16),
            pltpu.VMEM((2, 4, 4, 32, 128), BF16),
            pltpu.VMEM((4, 32, 128), F32),
            pltpu.VMEM((2, 4, 4, 4, 32, 128), BF16),
            pltpu.VMEM((2, 4, 240, 128), F32),
            pltpu.VMEM((2, 4, 240, 128), F32),
            pltpu.VMEM((2, 4, 240, 128), BF16),
            pltpu.VMEM((2, 4, 240, 128), BF16),
            pltpu.VMEM((2, 4, 240, 128), F32),
            pltpu.VMEM((2, 4, 64, 128), F32),
            pltpu.VMEM((2, 4, 64, 128), BF16),
            pltpu.VMEM((2, 4, 64, 128), BF16),
            pltpu.SemaphoreType.DMA((6,)),
            pltpu.SemaphoreType.DMA((N_SEMS,)),
            pltpu.SemaphoreType.DMA((N_SEMS,)),
        ],
        compiler_params=pltpu.CompilerParams(
            collective_id=0, has_side_effects=True, vmem_limit_bytes=60 * 2**20
        ),
    )(mask_in, mask_out, tokens, grad_out, weight_in, weight_out)


def solution(mesh):
    placed = (
        P("col", "row"),
        P("row", "col"),
        P("col", "row"),
        P("row", "col"),
        P("col", "row"),
        P("col", "row"),
    )
    return jax.shard_map(
        on_device,
        mesh=mesh,
        in_specs=placed,
        out_specs=(P("col", "row"), P("col", "row")),
        check_vma=False,
    )
```

time: 481 us -> 73.1 us (0.15); the launches traced: 474 us -> 72.8 us
  blocking collectives: 440 us -> 0 us
  Pallas kernels: 0 us -> 69.5 us
  starting transfers between devices: 11.9 us -> 0 us
  local copies, waits for them, and re-layouts: 13.9 us -> 2.69 us
  matrix products: 6.26 us -> 0 us
    unnamed x2 -> x0, blocking collectives: 258 us -> none
    all_gather x4 -> x0, blocking collectives: 182 us -> none  [the longest x1 63.4 us: on_device(): all_grads = lax.all_gather(grad_out, 'col', axis=0, tiled=True)]
    pallas_call x0 -> x1, Pallas kernels: none -> 69.5 us  [on_device(): pl.pallas_call(kernel, out_shape=(shape, shape), in_specs=[hbm] * 6, out_...]
    unnamed x6 -> x0, starting transfers between devices: 11.9 us -> none
    unnamed x32 -> x2, local copies, waits for them, and re-layouts: 13 us -> 2.69 us
    dot_general x4 -> x0, matrix products: 6.26 us -> none  [the longest x2 3.18 us: product_rows(): return jnp.dot(left, right, preferred_element_type=jnp.float32)]
  transfers between devices with their start and end apart: 6 -> 0, of which waited for: 0 -> 0; matrix products, arithmetic and copies ran while one was open for 1% -> 0% of each run, Pallas kernels for 0% -> 0%
where the time goes in v2:
time: 73.1 us; the launch traced here: 72.8 us
  Pallas kernels  69.5 us (95%)
  local copies, waits for them, and re-layouts  2.69 us (4%)
    pallas_call x1, Pallas kernels, on_device(): pl.pallas_call(kernel, out_shape=(shape, shape), in_specs=[hbm] * 6, out_...  69.5 us
    unnamed x2, local copies, waits for them, and re-layouts  2.69 us

profile of v2, /device:TPU:1, one launch (start us, length us, event | category | flops | bytes accessed | tf_op | source)
XLA Modules:
  0.0 72.8 jit_solution(16774656373571119684)
XLA Ops:
  0.6 69.5 %shard_map.77 = (bf16[10,768]{1,0:T(8,128)(2,1)}, bf16[10,768]{1,0:T(8,128)(2,1)}) custom-call(s32[6,6]{1,0:T(8,128)} %mask_in_hbm.1, s32[6,6]{1,0:T(8,128)} %mask_out_hbm.1, bf16[10,768]{1,0:T(8,128)(2,1)} %tok_hbm.1, bf16[10,768]{1,0:T(8,128)(2,1)} %grad_hbm.1, bf16[768,768]{1,0:T(8,128)(2,1)} %w_in_hbm.1, bf16[768,768]{1,0:T(8,128)(2,1)} %w_out_hbm.1), custom_call_target="tpu_custom_call" | custom-call | tf_op jit(solution)/shard_map/pallas_call | solution.py:264
  70.1 1.3 %copy.10 = bf16[10,768]{1,0:T(8,128)(2,1)} copy(bf16[10,768]{1,0:T(8,128)(2,1)} %get-tuple-element.4) | data formatting | bytes 30720
  71.5 1.3 %copy.11 = bf16[10,768]{1,0:T(8,128)(2,1)} copy(bf16[10,768]{1,0:T(8,128)(2,1)} %get-tuple-element.5) | data formatting | bytes 30720

commit v3 on v2

--- a/solution.py
+++ b/solution.py
@@ -9,15 +9,17 @@
 MESH = pl.DeviceIdType.MESH
 PLACES = (0, 1, 3, 2)
 ORDER = (
-    (1, 0, 0), (1, 1, 0), (0, 0, 1), (0, 0, 2), (0, 0, 3), (1, 0, 1), (0, 1, 1), (1, 0, 2),
-    (0, 1, 2), (1, 0, 3), (0, 1, 3), (1, 1, 1), (2, 0, 0), (1, 1, 2), (1, 1, 3), (2, 1, 0),
-    (2, 0, 1), (3, 0, 0), (2, 0, 2), (3, 1, 0), (2, 0, 3), (2, 1, 1), (3, 0, 1), (2, 1, 2),
-    (4, 0, 0), (3, 0, 2), (2, 1, 3), (4, 1, 0), (3, 0, 3), (3, 1, 1), (4, 0, 1), (3, 1, 2),
-    (5, 0, 0), (4, 0, 2), (3, 1, 3), (5, 1, 0), (6, 0, 0), (4, 0, 3), (4, 1, 1), (6, 1, 0),
-    (5, 0, 1), (4, 1, 2), (5, 0, 2), (6, 0, 1), (4, 1, 3), (5, 0, 3), (6, 0, 2), (5, 1, 1),
-    (6, 0, 3), (5, 1, 2), (6, 1, 1), (5, 1, 3), (6, 1, 2), (6, 1, 3), (7, 0, 0), (7, 1, 0),
+    (2, 0, 0), (2, 1, 0), (3, 0, 0), (3, 1, 0), (0, 0, 0), (0, 1, 0), (4, 0, 0), (2, 0, 1),
+    (2, 0, 2), (3, 0, 1), (4, 1, 0), (2, 1, 1), (1, 0, 3), (3, 0, 2), (2, 1, 2), (1, 1, 3),
+    (3, 1, 1), (3, 1, 2), (5, 0, 0), (2, 0, 3), (5, 1, 0), (4, 0, 1), (2, 1, 3), (3, 0, 3),
+    (4, 0, 2), (3, 1, 3), (6, 0, 0), (4, 1, 1), (6, 1, 0), (4, 1, 2), (5, 0, 1), (5, 0, 2),
+    (4, 0, 3), (5, 1, 1), (4, 1, 3), (5, 1, 2), (7, 0, 0), (6, 0, 1), (7, 1, 0), (6, 0, 2),
+    (8, 0, 0), (5, 0, 3), (8, 1, 0), (6, 1, 1), (5, 1, 3), (6, 1, 2), (7, 0, 1), (9, 0, 0),
+    (7, 0, 2), (6, 0, 3), (8, 0, 1), (9, 1, 0), (7, 1, 1), (8, 0, 2), (6, 1, 3), (7, 1, 2),
+    (8, 1, 1), (8, 1, 2), (9, 0, 1), (7, 0, 3), (9, 0, 2), (7, 1, 3), (8, 0, 3), (9, 1, 1),
+    (8, 1, 3), (9, 1, 2), (9, 0, 3), (9, 1, 3),
 )
-N_SEMS = 34 + 8 * 21 + 20
+N_SEMS = 40 + 8 * 21 + 38
 
 
 def nn(a, b):
@@ -106,23 +108,39 @@
         for j in range(6):
             pack[a, pl.ds(j, 10, stride=6), :] = v[:, 128 * j : 128 * (j + 1)]
         gath[a, 0, 0, 0] = pack[a].astype(BF16)
-        for e in range(4):
-            piece[a, e, pl.ds(56, 8), :] = jnp.zeros((8, 128), F32)
+        for p in range(4):
+            for e in range(4):
+                piece[a, p, e, pl.ds(56, 8), :] = jnp.zeros((8, 128), F32)
     pl.semaphore_wait(barrier, len(peers))
 
     near, far, xs, sibs = {}, {}, {}, {}
-
-    def spread(a, lo, hi):
-        src = gath.at[a, 0, 0, pl.ds(lo, hi - lo)]
-        for d in (1, 3, 2):
-            dst = gath.at[a, 4 - d, 0, pl.ds(lo, hi - lo)]
-            xs.setdefault((a, 4 - d), []).append(put(src, dst, at_x(d)))
+    ys, zls, gz, gy, pairs, xr, zr = {}, {}, {}, {}, {}, {}, {0: [], 1: []}
+
+    def spread(a, p):
+        xs[a, p] = [put(gath.at[a, p, 0, 0], gath.at[a, p, 0, 4 - e], at_x(e)) for e in (2, 1, 3)]
+
+    def from_near(a, _):
+        top, low = pl.ds(0, 32), pl.ds(32, 32)
+        arrive(near[a][1:])
+        far[a] = [put(gath.at[a, 1, 0, 0, top], gath.at[a, 3, 0, 0, top], at_zh(3))]
+        arrive(near[a][:1])
+        far[a].append(put(gath.at[a, 2, 0, 0, low], gath.at[a, 3, 0, 0, low], at_zh(1)))
+        spread(a, 1)
+        spread(a, 2)
+
+    def from_far(a, p):
+        arrive(far[a])
+        spread(a, p)
+
+    def to_sibling(a, p):
+        arrive(xs[a, p])
+        sibs[a, p] = put(gath.at[a, p, 0], gath.at[a, p, 1], sibling)
 
     for a in (0, 1):
         own = gath.at[a, 0, 0, 0]
-        near[a] = [put(own, gath.at[a, 0, 0, 2], at_zh(1)), put(own, gath.at[a, 0, 0, 1], at_zh(3))]
+        near[a] = [put(own, gath.at[a, 2, 0, 0], at_zh(1)), put(own, gath.at[a, 1, 0, 0], at_zh(3))]
     for a in (0, 1):
-        spread(a, 0, 1)
+        spread(a, 0)
     for load in loads[2:]:
         load.wait()
     for w, mask in ((w_in, mask_in), (w_out, mask_out)):
@@ -132,24 +150,6 @@
                 cols = slice(128 * j, 128 * (j + 1))
                 keep = mask[i, j].astype(F32)
                 w[rows, cols] = (w[rows, cols].astype(F32) * keep).astype(BF16)
-    for a in (0, 1):
-        arrive(near[a])
-        top, low = pl.ds(0, 32), pl.ds(32, 32)
-        far[a] = [
-            put(gath.at[a, 0, 0, 1, top], gath.at[a, 0, 0, 3, top], at_zh(3)),
-            put(gath.at[a, 0, 0, 2, low], gath.at[a, 0, 0, 3, low], at_zh(1)),
-        ]
-        spread(a, 1, 3)
-    for a in (0, 1):
-        arrive(far[a])
-        sibs[a, 0] = put(gath.at[a, 0, 0], gath.at[a, 0, 1], sibling)
-        spread(a, 3, 4)
-
-    ys, zls, gz, gy, pairs, xr, zr = {}, {}, {}, {}, {}, {}, {}
-
-    def to_sibling(a, d):
-        arrive(xs[a, d])
-        sibs[a, d] = put(gath.at[a, d, 0], gath.at[a, d, 1], sibling)
 
     def first_product(a, d):
         arrive([sibs[a, d]])
@@ -165,7 +165,7 @@
             part_f[a, d, g] = part
             part_b[a, d, g] = part.astype(BF16)
         ys[a, d] = [
-            put(part_b.at[a, d, (y + e) % 4], y_in.at[a, d, 4 - e], at_y(e)) for e in (1, 3, 2)
+            put(part_b.at[a, d, (y + e) % 4], y_in.at[a, d, 4 - e], at_y(e)) for e in (2, 1, 3)
         ]
 
     def sum_over_y(a, d):
@@ -216,42 +216,41 @@
 
     def sum_over_cores(a, d):
         arrive([pairs[a, d]])
-        total = mine[a, d] + sib_in[a, d]
-        if d:
-            x_out[a, d] = total.astype(BF16)
-            xr[a, d] = put(x_out.at[a, d], x_in.at[a, 4 - d], at_x(d))
+        mine[a, d] = mine[a, d] + sib_in[a, d]
+        xr[a, d] = []
+        for e in (2, 1, 3, 0):
+            for j in range(6):
+                piece[a, d, e, pl.ds(10 * j, 10), :] = mine[a, d, pl.ds(40 * j + 10 * e, 10), :]
+            if e:
+                x_out[a, d, e] = piece[a, d, e].astype(BF16)
+                xr[a, d].append(put(x_out.at[a, d, e], x_in.at[a, d, 4 - e], at_x(e)))
+
+    def sum_over_x(a, p):
+        arrive(xr[a, p])
+        total = piece[a, p, 0]
+        for e in (1, 2, 3):
+            total = total + x_in[a, p, e].astype(F32)
+        e = PLACES[p]
+        if e:
+            zh_out[a, e] = total.astype(BF16)
+            zr[a].append(put(zh_out.at[a, e], zh_in.at[a, 4 - e], at_zh(e)))
         else:
-            mine[a, 0] = total
-
-    def sum_over_x(a, _):
-        arrive([xr[a, d] for d in (1, 2, 3)])
-        total = mine[a, 0]
-        for d in (1, 2, 3):
-            total = total + x_in[a, d].astype(F32)
-        mine[a, 0] = total
-        zr[a] = []
-        for p in (3, 1, 2, 0):
-            e = PLACES[p]
-            for j in range(6):
-                piece[a, p, pl.ds(10 * j, 10), :] = mine[a, 0, pl.ds(40 * j + 10 * p, 10), :]
-            if e:
-                zh_out[a, p] = piece[a, p].astype(BF16)
-                zr[a].append(put(zh_out.at[a, p], zh_in.at[a, 4 - e], at_zh(e)))
+            piece[a, 0, 0] = total
 
     stages = (
-        to_sibling, first_product, sum_over_y, activate, pass_on, second_product,
-        sum_over_cores, sum_over_x,
+        from_near, from_far, to_sibling, first_product, sum_over_y, activate, pass_on,
+        second_product, sum_over_cores, sum_over_x,
     )
-    for stage, a, d in ORDER:
-        stages[stage](a, d)
+    for stage, a, p in ORDER:
+        stages[stage](a, p)
     for a, ref in ((0, out), (1, gtok)):
         arrive(zr[a])
-        total = piece[a, 0]
+        total = piece[a, 0, 0]
         for e in (1, 2, 3):
             total = total + zh_in[a, e].astype(F32)
-        piece[a, 0] = total
+        piece[a, 0, 0] = total
         ref[...] = jnp.concatenate(
-            [piece[a, 0, pl.ds(10 * j, 10), :] for j in range(6)], axis=1
+            [piece[a, 0, 0, pl.ds(10 * j, 10), :] for j in range(6)], axis=1
         ).astype(BF16)
     for copy in started:
         copy.wait_send()
@@ -286,10 +285,10 @@
             pltpu.VMEM((2, 4, 4, 4, 32, 128), BF16),
             pltpu.VMEM((2, 4, 240, 128), F32),
             pltpu.VMEM((2, 4, 240, 128), F32),
-            pltpu.VMEM((2, 4, 240, 128), BF16),
-            pltpu.VMEM((2, 4, 240, 128), BF16),
+            pltpu.VMEM((2, 4, 4, 64, 128), BF16),
+            pltpu.VMEM((2, 4, 4, 64, 128), BF16),
             pltpu.VMEM((2, 4, 240, 128), F32),
-            pltpu.VMEM((2, 4, 64, 128), F32),
+            pltpu.VMEM((2, 4, 4, 64, 128), F32),
             pltpu.VMEM((2, 4, 64, 128), BF16),
             pltpu.VMEM((2, 4, 64, 128), BF16),
             pltpu.SemaphoreType.DMA((6,)),

time: 73.1 us -> 70.7 us (0.967)
  Pallas kernels: 69.5 us -> 67.1 us
    pallas_call x1, Pallas kernels: 69.5 us -> 67.1 us  [on_device(): pl.pallas_call(kernel, out_shape=(shape, shape), in_specs=[hbm] * 6, out_...]
where the time goes in v3:
time: 70.7 us; the launch traced here: 70.4 us
  Pallas kernels  67.1 us (95%)
  local copies, waits for them, and re-layouts  2.69 us (4%)
    pallas_call x1, Pallas kernels, on_device(): pl.pallas_call(kernel, out_shape=(shape, shape), in_specs=[hbm] * 6, out_...  67.1 us
    unnamed x2, local copies, waits for them, and re-layouts  2.69 us

profile of v3, /device:TPU:1, one launch (start us, length us, event | category | flops | bytes accessed | tf_op | source)
XLA Modules:
  0.0 70.4 jit_solution(8583030058273431169)
XLA Ops:
  0.6 67.1 %shard_map.77 = (bf16[10,768]{1,0:T(8,128)(2,1)}, bf16[10,768]{1,0:T(8,128)(2,1)}) custom-call(s32[6,6]{1,0:T(8,128)} %mask_in_hbm.1, s32[6,6]{1,0:T(8,128)} %mask_out_hbm.1, bf16[10,768]{1,0:T(8,128)(2,1)} %tok_hbm.1, bf16[10,768]{1,0:T(8,128)(2,1)} %grad_hbm.1, bf16[768,768]{1,0:T(8,128)(2,1)} %w_in_hbm.1, bf16[768,768]{1,0:T(8,128)(2,1)} %w_out_hbm.1), custom_call_target="tpu_custom_call" | custom-call | tf_op jit(solution)/shard_map/pallas_call | solution.py:263
  67.8 1.3 %copy.10 = bf16[10,768]{1,0:T(8,128)(2,1)} copy(bf16[10,768]{1,0:T(8,128)(2,1)} %get-tuple-element.4) | data formatting | bytes 30720
  69.1 1.3 %copy.11 = bf16[10,768]{1,0:T(8,128)(2,1)} copy(bf16[10,768]{1,0:T(8,128)(2,1)} %get-tuple-element.5) | data formatting | bytes 30720

commit v4 on v3

--- a/solution.py
+++ b/solution.py
@@ -19,7 +19,7 @@
     (8, 1, 1), (8, 1, 2), (9, 0, 1), (7, 0, 3), (9, 0, 2), (7, 1, 3), (8, 0, 3), (9, 1, 1),
     (8, 1, 3), (9, 1, 2), (9, 0, 3), (9, 1, 3),
 )
-N_SEMS = 40 + 8 * 21 + 38
+NEAR, FAR, XS, SIB, YS, ZS, GZ, GY, PAIR, XR, ZR = range(11)
 
 
 def nn(a, b):
@@ -42,10 +42,11 @@
 
 
 def kernel(
-    mask_in_hbm, mask_out_hbm, tok_hbm, grad_hbm, w_in_hbm, w_out_hbm, out, gtok,
+    mask_in_hbm, mask_out_hbm, tok_hbm, grad_hbm, w_in_hbm, w_out_hbm, out,
     mask_in, mask_out, tok, grad, w_in, w_out, gath, pack, unp, part_f, part_b, y_in,
     half_f, half_b, z_in, pre_s, hid, sib_out, sib_in, x_out, x_in, mine, piece, zh_out, zh_in,
-    load_sem, send, recv,
+    load_sem, send, got_near, got_far, got_x, got_sib, got_y, got_z, got_gz, got_gy, got_pair, got_xr,
+    got_zr,
 ):
     r, c = lax.axis_index("row"), lax.axis_index("col")
     zl, y = r // 4, r % 4
@@ -85,21 +86,14 @@
         loads.append(pltpu.make_async_copy(src, dst, load_sem.at[len(loads)]))
         loads[-1].start()
 
-    started = []
-
-    def put(src, dst, peer):
-        i = len(started)
-        copy = pltpu.make_async_remote_copy(
-            src_ref=src, dst_ref=dst, send_sem=send.at[i], recv_sem=recv.at[i],
+    def put(src, dst, peer, kind, sem):
+        pltpu.make_async_remote_copy(
+            src_ref=src, dst_ref=dst, send_sem=send.at[kind], recv_sem=sem,
             device_id=peer, device_id_type=MESH,
-        )
-        copy.start()
-        started.append(copy)
-        return copy
-
-    def arrive(copies):
-        for copy in copies:
-            copy.wait_recv()
+        ).start()
+
+    def arrive(ref, sem):
+        pltpu.make_async_copy(ref, ref, sem).wait()
 
     for a, v in ((0, tok), (1, grad)):
         loads[a].wait()
@@ -113,32 +107,32 @@
                 piece[a, p, e, pl.ds(56, 8), :] = jnp.zeros((8, 128), F32)
     pl.semaphore_wait(barrier, len(peers))
 
-    near, far, xs, sibs = {}, {}, {}, {}
-    ys, zls, gz, gy, pairs, xr, zr = {}, {}, {}, {}, {}, {}, {0: [], 1: []}
-
     def spread(a, p):
-        xs[a, p] = [put(gath.at[a, p, 0, 0], gath.at[a, p, 0, 4 - e], at_x(e)) for e in (2, 1, 3)]
+        for e in (2, 1, 3):
+            put(gath.at[a, p, 0, 0], gath.at[a, p, 0, 4 - e], at_x(e), XS, got_x.at[a, p])
 
     def from_near(a, _):
         top, low = pl.ds(0, 32), pl.ds(32, 32)
-        arrive(near[a][1:])
-        far[a] = [put(gath.at[a, 1, 0, 0, top], gath.at[a, 3, 0, 0, top], at_zh(3))]
-        arrive(near[a][:1])
-        far[a].append(put(gath.at[a, 2, 0, 0, low], gath.at[a, 3, 0, 0, low], at_zh(1)))
+        far = gath.at[a, 3, 0, 0]
+        arrive(gath.at[a, 1, 0, 0], got_near.at[a, 1])
+        put(gath.at[a, 1, 0, 0, top], far.at[top], at_zh(3), FAR, got_far.at[a])
+        arrive(gath.at[a, 2, 0, 0], got_near.at[a, 0])
+        put(gath.at[a, 2, 0, 0, low], far.at[low], at_zh(1), FAR, got_far.at[a])
         spread(a, 1)
         spread(a, 2)
 
     def from_far(a, p):
-        arrive(far[a])
+        arrive(gath.at[a, 3, 0, 0], got_far.at[a])
         spread(a, p)
 
     def to_sibling(a, p):
-        arrive(xs[a, p])
-        sibs[a, p] = put(gath.at[a, p, 0], gath.at[a, p, 1], sibling)
+        arrive(gath.at[a, p, 0, pl.ds(1, 3)], got_x.at[a, p])
+        put(gath.at[a, p, 0], gath.at[a, p, 1], sibling, SIB, got_sib.at[a, p])
 
     for a in (0, 1):
         own = gath.at[a, 0, 0, 0]
-        near[a] = [put(own, gath.at[a, 2, 0, 0], at_zh(1)), put(own, gath.at[a, 1, 0, 0], at_zh(3))]
+        put(own, gath.at[a, 2, 0, 0], at_zh(1), NEAR, got_near.at[a, 0])
+        put(own, gath.at[a, 1, 0, 0], at_zh(3), NEAR, got_near.at[a, 1])
     for a in (0, 1):
         spread(a, 0)
     for load in loads[2:]:
@@ -152,24 +146,23 @@
                 w[rows, cols] = (w[rows, cols].astype(F32) * keep).astype(BF16)
 
     def first_product(a, d):
-        arrive([sibs[a, d]])
+        arrive(gath.at[a, d, 1], got_sib.at[a, d])
         for s in range(8):
             unp[a, pl.ds(60 * s, 60), :] = gath[a, d, s // 4, s % 4].astype(F32)[:60]
         left = jnp.concatenate(
             [unp[a, pl.ds(j, 80, stride=6), :].astype(BF16) for j in range(6)], axis=1
-        )
+        ).astype(BF16)
         value = nn(left, w_in[...]) if a == 0 else nt(left, w_out[...])
         rows = jnp.concatenate([lanes_to_rows(value), jnp.zeros((32, 128), F32)], axis=0)
         for g in range(4):
             part = rows[128 * g : 128 * (g + 1)]
             part_f[a, d, g] = part
             part_b[a, d, g] = part.astype(BF16)
-        ys[a, d] = [
-            put(part_b.at[a, d, (y + e) % 4], y_in.at[a, d, 4 - e], at_y(e)) for e in (2, 1, 3)
-        ]
+        for e in (2, 1, 3):
+            put(part_b.at[a, d, (y + e) % 4], y_in.at[a, d, 4 - e], at_y(e), YS, got_y.at[a, d])
 
     def sum_over_y(a, d):
-        arrive(ys[a, d])
+        arrive(y_in.at[a, d, pl.ds(1, 3)], got_y.at[a, d])
         total = part_f[a, d, y]
         for e in (1, 2, 3):
             total = total + y_in[a, d, e].astype(F32)
@@ -177,12 +170,11 @@
             rows = total[32 * q : 32 * (q + 1)]
             half_f[a, d, q] = rows
             half_b[a, d, q] = rows.astype(BF16)
-        zls[a, d] = [
-            put(half_b.at[a, d, (zl + e) % 4], z_in.at[a, d, 4 - e], at_zl(e)) for e in (2, 1, 3)
-        ]
+        for e in (2, 1, 3):
+            put(half_b.at[a, d, (zl + e) % 4], z_in.at[a, d, 4 - e], at_zl(e), ZS, got_z.at[a, d])
 
     def activate(a, d):
-        arrive(zls[a, d])
+        arrive(z_in.at[a, d, pl.ds(1, 3)], got_z.at[a, d])
         total = half_f[a, d, zl]
         for e in (1, 2, 3):
             total = total + z_in[a, d, e].astype(F32)
@@ -196,44 +188,46 @@
             value = (s + v * (s * (1.0 - s)) * slope) * total
         hid[a, d, y, zl] = value.astype(BF16)
         slot = hid.at[a, d, y, zl]
-        gz[a, d] = [put(slot, slot, at_zl(e)) for e in (1, 2, 3)]
-        gy[a, d] = [put(slot, slot, at_y(e)) for e in (1, 3, 2)]
+        for e in (1, 2, 3):
+            put(slot, slot, at_zl(e), GZ, got_gz.at[a, d, e])
+        for e in (1, 3, 2):
+            put(slot, slot, at_y(e), GY, got_gy.at[a, d])
 
     def pass_on(a, d):
         for e in (1, 2, 3):
-            arrive([gz[a, d][e - 1]])
             slot = hid.at[a, d, y, (zl + 4 - e) % 4]
-            gy[a, d] += [put(slot, slot, at_y(f)) for f in (1, 3, 2)]
+            arrive(slot, got_gz.at[a, d, e])
+            for f in (1, 3, 2):
+                put(slot, slot, at_y(f), GY, got_gy.at[a, d])
 
     def second_product(a, d):
-        arrive(gy[a, d])
+        arrive(hid.at[a, d, pl.ds(0, 3)], got_gy.at[a, d])
         rows = hid[a, d].reshape(512, 128)
         left = jnp.concatenate([rows[80 * j : 80 * (j + 1)] for j in range(6)], axis=1)
         value = nn(left, w_out[...]) if a == 0 else nt(left, w_in[...])
         mine[a, d] = lanes_to_rows(value[:40])
         sib_out[a, d] = lanes_to_rows(value[40:])
-        pairs[a, d] = put(sib_out.at[a, d], sib_in.at[a, d], sibling)
+        put(sib_out.at[a, d], sib_in.at[a, d], sibling, PAIR, got_pair.at[a, d])
 
     def sum_over_cores(a, d):
-        arrive([pairs[a, d]])
+        arrive(sib_in.at[a, d], got_pair.at[a, d])
         mine[a, d] = mine[a, d] + sib_in[a, d]
-        xr[a, d] = []
         for e in (2, 1, 3, 0):
             for j in range(6):
                 piece[a, d, e, pl.ds(10 * j, 10), :] = mine[a, d, pl.ds(40 * j + 10 * e, 10), :]
             if e:
                 x_out[a, d, e] = piece[a, d, e].astype(BF16)
-                xr[a, d].append(put(x_out.at[a, d, e], x_in.at[a, d, 4 - e], at_x(e)))
+                put(x_out.at[a, d, e], x_in.at[a, d, 4 - e], at_x(e), XR, got_xr.at[a, d])
 
     def sum_over_x(a, p):
-        arrive(xr[a, p])
+        arrive(x_in.at[a, p, pl.ds(1, 3)], got_xr.at[a, p])
         total = piece[a, p, 0]
         for e in (1, 2, 3):
             total = total + x_in[a, p, e].astype(F32)
         e = PLACES[p]
         if e:
             zh_out[a, e] = total.astype(BF16)
-            zr[a].append(put(zh_out.at[a, e], zh_in.at[a, 4 - e], at_zh(e)))
+            put(zh_out.at[a, e], zh_in.at[a, 4 - e], at_zh(e), ZR, got_zr.at[a])
         else:
             piece[a, 0, 0] = total
 
@@ -243,28 +237,41 @@
     )
     for stage, a, p in ORDER:
         stages[stage](a, p)
-    for a, ref in ((0, out), (1, gtok)):
-        arrive(zr[a])
+    for a in (0, 1):
+        arrive(zh_in.at[a, pl.ds(1, 3)], got_zr.at[a])
         total = piece[a, 0, 0]
         for e in (1, 2, 3):
             total = total + zh_in[a, e].astype(F32)
         piece[a, 0, 0] = total
-        ref[...] = jnp.concatenate(
+        out[a] = jnp.concatenate(
             [piece[a, 0, 0, pl.ds(10 * j, 10), :] for j in range(6)], axis=1
         ).astype(BF16)
-    for copy in started:
-        copy.wait_send()
+    every = slice(None)
+    for kind, ref in (
+        (NEAR, gath.at[0, 0, 0]),
+        (FAR, gath.at[0, 0, 0, pl.ds(0, 2)]),
+        (XS, gath.at[every, every, 0, pl.ds(1, 3)]),
+        (SIB, gath.at[every, every, 0]),
+        (YS, y_in.at[every, every, pl.ds(1, 3)]),
+        (ZS, z_in.at[every, every, pl.ds(1, 3)]),
+        (GZ, z_in.at[every, every, pl.ds(1, 3)]),
+        (GY, hid.at[every, every, pl.ds(0, 3)]),
+        (PAIR, sib_in),
+        (XR, x_in.at[every, every, pl.ds(1, 3)]),
+        (ZR, zh_in.at[every, pl.ds(1, 3)]),
+    ):
+        arrive(ref, send.at[kind])
 
 
 def on_device(tokens, weight_in, weight_out, mask_in, mask_out, grad_out):
     vmem = pl.BlockSpec(memory_space=pltpu.VMEM)
     hbm = pl.BlockSpec(memory_space=pltpu.HBM)
-    shape = jax.ShapeDtypeStruct(tokens.shape, BF16)
-    return pl.pallas_call(
+    shape = jax.ShapeDtypeStruct((2,) + tokens.shape, BF16)
+    o = pl.pallas_call(
         kernel,
-        out_shape=(shape, shape),
+        out_shape=shape,
         in_specs=[hbm] * 6,
-        out_specs=(vmem, vmem),
+        out_specs=vmem,
         scratch_shapes=[
             pltpu.SMEM(mask_in.shape, jnp.int32),
             pltpu.SMEM(mask_out.shape, jnp.int32),
@@ -292,13 +299,24 @@
             pltpu.VMEM((2, 4, 64, 128), BF16),
             pltpu.VMEM((2, 4, 64, 128), BF16),
             pltpu.SemaphoreType.DMA((6,)),
-            pltpu.SemaphoreType.DMA((N_SEMS,)),
-            pltpu.SemaphoreType.DMA((N_SEMS,)),
+            pltpu.SemaphoreType.DMA((11,)),
+            pltpu.SemaphoreType.DMA((2, 2)),
+            pltpu.SemaphoreType.DMA((2,)),
+            pltpu.SemaphoreType.DMA((2, 4)),
+            pltpu.SemaphoreType.DMA((2, 4)),
+            pltpu.SemaphoreType.DMA((2, 4)),
+            pltpu.SemaphoreType.DMA((2, 4)),
+            pltpu.SemaphoreType.DMA((2, 4, 4)),
+            pltpu.SemaphoreType.DMA((2, 4)),
+            pltpu.SemaphoreType.DMA((2, 4)),
+            pltpu.SemaphoreType.DMA((2, 4)),
+            pltpu.SemaphoreType.DMA((2,)),
         ],
         compiler_params=pltpu.CompilerParams(
             collective_id=0, has_side_effects=True, vmem_limit_bytes=60 * 2**20
         ),
     )(mask_in, mask_out, tokens, grad_out, weight_in, weight_out)
+    return o[0], o[1]
 
 
 def solution(mesh):

time: 70.7 us -> 65.5 us (0.926)
  Pallas kernels: 67.1 us -> 63.3 us
  local copies, waits for them, and re-layouts: 2.69 us -> 1.38 us
    pallas_call x1, Pallas kernels: 67.1 us -> 63.3 us  [on_device(): pl.pallas_call(kernel, out_shape=shape, in_specs=[hbm] * 6, out_specs=vme...]
    unnamed x2 -> x0, local copies, waits for them, and re-layouts: 2.69 us -> none
    squeeze x0 -> x1, local copies, waits for them, and re-layouts: none -> 1.38 us  [on_device(): return (o[0], o[1])]
where the time goes in v4:
time: 65.5 us; the launch traced here: 65.3 us
  Pallas kernels  63.3 us (97%)
  local copies, waits for them, and re-layouts  1.38 us (2%)
    pallas_call x1, Pallas kernels, on_device(): pl.pallas_call(kernel, out_shape=shape, in_specs=[hbm] * 6, out_specs=vme...  63.3 us
    squeeze x1, local copies, waits for them, and re-layouts, on_device(): return (o[0], o[1])  1.38 us

profile of v4, /device:TPU:1, one launch (start us, length us, event | category | flops | bytes accessed | tf_op | source)
XLA Modules:
  0.0 65.3 jit_solution(1830004009317312768)
XLA Ops:
  0.6 63.3 %shard_map.77 = bf16[2,10,768]{2,1,0:T(8,128)(2,1)} custom-call(s32[6,6]{1,0:T(8,128)} %mask_in_hbm.1, s32[6,6]{1,0:T(8,128)} %mask_out_hbm.1, bf16[10,768]{1,0:T(8,128)(2,1)} %tok_hbm.1, bf16[10,768]{1,0:T(8,128)(2,1)} %grad_hbm.1, bf16[768,768]{1,0:T(8,128)(2,1)} %w_in_hbm.1, bf16[768,768]{1,0:T(8,128)(2,1)} %w_out_hbm.1), custom_call_target="tpu_custom_call" | custom-call | tf_op jit(solution)/shard_map/pallas_call | solution.py:270
  63.9 1.4 %slice_bitcast_fusion = (bf16[10,768]{1,0:T(8,128)(2,1)}, bf16[10,768]{1,0:T(8,128)(2,1)}) fusion(bf16[2,10,768]{2,1,0:T(8,128)(2,1)} %shard_map.77), kind=kLoop, calls=%fused_computation | loop fusion | bytes 61440 | tf_op jit(solution)/shard_map/squeeze | solution.py:319

commit v5 on v4

--- a/solution.py
+++ b/solution.py
@@ -9,17 +9,18 @@
 MESH = pl.DeviceIdType.MESH
 PLACES = (0, 1, 3, 2)
 ORDER = (
-    (2, 0, 0), (2, 1, 0), (3, 0, 0), (3, 1, 0), (0, 0, 0), (0, 1, 0), (4, 0, 0), (2, 0, 1),
-    (2, 0, 2), (3, 0, 1), (4, 1, 0), (2, 1, 1), (1, 0, 3), (3, 0, 2), (2, 1, 2), (1, 1, 3),
-    (3, 1, 1), (3, 1, 2), (5, 0, 0), (2, 0, 3), (5, 1, 0), (4, 0, 1), (2, 1, 3), (3, 0, 3),
-    (4, 0, 2), (3, 1, 3), (6, 0, 0), (4, 1, 1), (6, 1, 0), (4, 1, 2), (5, 0, 1), (5, 0, 2),
-    (4, 0, 3), (5, 1, 1), (4, 1, 3), (5, 1, 2), (7, 0, 0), (6, 0, 1), (7, 1, 0), (6, 0, 2),
-    (8, 0, 0), (5, 0, 3), (8, 1, 0), (6, 1, 1), (5, 1, 3), (6, 1, 2), (7, 0, 1), (9, 0, 0),
-    (7, 0, 2), (6, 0, 3), (8, 0, 1), (9, 1, 0), (7, 1, 1), (8, 0, 2), (6, 1, 3), (7, 1, 2),
-    (8, 1, 1), (8, 1, 2), (9, 0, 1), (7, 0, 3), (9, 0, 2), (7, 1, 3), (8, 0, 3), (9, 1, 1),
-    (8, 1, 3), (9, 1, 2), (9, 0, 3), (9, 1, 3),
+    (3, 0, 0), (0, 0, 0), (4, 0, 0), (0, 1, 0), (3, 1, 0), (1, 0, 0), (1, 1, 0), (4, 1, 0),
+    (2, 0, 3), (3, 0, 1), (5, 0, 0), (3, 0, 2), (4, 0, 1), (2, 1, 3), (4, 0, 2), (5, 1, 0),
+    (3, 1, 2), (3, 1, 1), (6, 0, 0), (4, 0, 3), (4, 1, 1), (4, 1, 3), (4, 1, 2), (6, 1, 0),
+    (5, 0, 1), (5, 0, 2), (5, 0, 3), (5, 1, 3), (5, 1, 2), (5, 1, 1), (7, 1, 0), (6, 0, 2),
+    (6, 0, 3), (6, 0, 1), (6, 1, 3), (6, 1, 2), (6, 1, 1), (7, 0, 2), (7, 0, 3), (7, 0, 1),
+    (7, 1, 3), (7, 1, 1), (7, 1, 2), (7, 0, 0), (8, 1, 0), (8, 0, 2), (8, 0, 3), (9, 0, 2),
+    (8, 0, 1), (8, 1, 3), (9, 1, 0), (8, 1, 2), (8, 1, 1), (9, 0, 1), (10, 0, 3), (8, 0, 0),
+    (9, 1, 2), (9, 1, 1), (10, 0, 2), (10, 1, 3), (10, 0, 1), (9, 0, 0), (10, 1, 2), (10, 1, 0),
+    (10, 1, 1), (10, 0, 0),
 )
-NEAR, FAR, XS, SIB, YS, ZS, GZ, GY, PAIR, XR, ZR = range(11)
+NEAR, FAR, XS, SIB, FIRST, SECOND, GATHER, SPREAD, PAIR, XR, ZR, CROSS_IN, CROSS_OUT = range(13)
+Z_FIRST = ((0, 1), (1, 1))
 
 
 def nn(a, b):
@@ -44,7 +45,8 @@
 def kernel(
     mask_in_hbm, mask_out_hbm, tok_hbm, grad_hbm, w_in_hbm, w_out_hbm, out,
     mask_in, mask_out, tok, grad, w_in, w_out, gath, pack, unp, part_f, part_b, y_in,
-    half_f, half_b, z_in, pre_s, hid, sib_out, sib_in, x_out, x_in, mine, piece, zh_out, zh_in,
+    half_f, half_b, z_in, pre_s, hid, sib_out, sib_in, x_out, x_in, mine, piece, cross,
+    cross_out, cross_in, zh_out, zh_in,
     load_sem, send, got_near, got_far, got_x, got_sib, got_y, got_z, got_gz, got_gy, got_pair, got_xr,
     got_zr,
 ):
@@ -64,7 +66,15 @@
     def at_zh(d):
         return {"col": ((zh + d) % 4) * 8 + x * 2 + k}
 
-    sibling = {"col": zh * 8 + x * 2 + (1 - k)}
+    def at_cross(d):
+        return {"col": zh * 8 + ((x + d) % 4) * 2 + (1 - k)}
+
+    def axes(a, p):
+        if (a, p) in Z_FIRST:
+            return zl, at_zl, y, at_y
+        return y, at_y, zl, at_zl
+
+    sibling = at_cross(0)
 
     barrier = pltpu.get_barrier_semaphore()
     peers = [at_zh(1), at_zh(3)]
@@ -103,6 +113,7 @@
             pack[a, pl.ds(j, 10, stride=6), :] = v[:, 128 * j : 128 * (j + 1)]
         gath[a, 0, 0, 0] = pack[a].astype(BF16)
         for p in range(4):
+            cross[a, p, pl.ds(56, 8), :] = jnp.zeros((8, 128), F32)
             for e in range(4):
                 piece[a, p, e, pl.ds(56, 8), :] = jnp.zeros((8, 128), F32)
     pl.semaphore_wait(barrier, len(peers))
@@ -110,15 +121,25 @@
     def spread(a, p):
         for e in (2, 1, 3):
             put(gath.at[a, p, 0, 0], gath.at[a, p, 0, 4 - e], at_x(e), XS, got_x.at[a, p])
+            if p == 3:
+                dst = gath.at[a, 3, 1, 4 - e]
+                put(gath.at[a, 3, 0, 0], dst, at_cross(e), CROSS_IN, got_sib.at[a, 3])
+        if p == 3:
+            put(gath.at[a, 3, 0, 0], gath.at[a, 3, 1, 0], sibling, CROSS_IN, got_sib.at[a, 3])
+
+    top, low = pl.ds(0, 32), pl.ds(32, 32)
+
+    def relay(a, _):
+        far = gath.at[a, 3, 0, 0]
+        arrive(gath.at[a, 1, 0, 0, top], got_near.at[a, 0])
+        put(gath.at[a, 1, 0, 0, top], far.at[top], at_zh(3), FAR, got_far.at[a])
+        arrive(gath.at[a, 2, 0, 0, low], got_near.at[a, 1])
+        put(gath.at[a, 2, 0, 0, low], far.at[low], at_zh(1), FAR, got_far.at[a])
 
     def from_near(a, _):
-        top, low = pl.ds(0, 32), pl.ds(32, 32)
-        far = gath.at[a, 3, 0, 0]
-        arrive(gath.at[a, 1, 0, 0], got_near.at[a, 1])
-        put(gath.at[a, 1, 0, 0, top], far.at[top], at_zh(3), FAR, got_far.at[a])
-        arrive(gath.at[a, 2, 0, 0], got_near.at[a, 0])
-        put(gath.at[a, 2, 0, 0, low], far.at[low], at_zh(1), FAR, got_far.at[a])
+        arrive(gath.at[a, 1, 0, 0, low], got_near.at[a, 2])
         spread(a, 1)
+        arrive(gath.at[a, 2, 0, 0, top], got_near.at[a, 3])
         spread(a, 2)
 
     def from_far(a, p):
@@ -129,10 +150,11 @@
         arrive(gath.at[a, p, 0, pl.ds(1, 3)], got_x.at[a, p])
         put(gath.at[a, p, 0], gath.at[a, p, 1], sibling, SIB, got_sib.at[a, p])
 
-    for a in (0, 1):
-        own = gath.at[a, 0, 0, 0]
-        put(own, gath.at[a, 2, 0, 0], at_zh(1), NEAR, got_near.at[a, 0])
-        put(own, gath.at[a, 1, 0, 0], at_zh(3), NEAR, got_near.at[a, 1])
+    for i, halves in ((0, (top, low)), (2, (low, top))):
+        for a in (0, 1):
+            own = gath.at[a, 0, 0, 0]
+            for j, p, half, e in ((i, 1, halves[0], 3), (i + 1, 2, halves[1], 1)):
+                put(own.at[half], gath.at[a, p, 0, 0, half], at_zh(e), NEAR, got_near.at[a, j])
     for a in (0, 1):
         spread(a, 0)
     for load in loads[2:]:
@@ -146,6 +168,8 @@
                 w[rows, cols] = (w[rows, cols].astype(F32) * keep).astype(BF16)
 
     def first_product(a, d):
+        if d == 3:
+            arrive(gath.at[a, 3, 0, pl.ds(1, 3)], got_x.at[a, 3])
         arrive(gath.at[a, d, 1], got_sib.at[a, d])
         for s in range(8):
             unp[a, pl.ds(60 * s, 60), :] = gath[a, d, s // 4, s % 4].astype(F32)[:60]
@@ -158,12 +182,14 @@
             part = rows[128 * g : 128 * (g + 1)]
             part_f[a, d, g] = part
             part_b[a, d, g] = part.astype(BF16)
+        i, at, _, _ = axes(a, d)
         for e in (2, 1, 3):
-            put(part_b.at[a, d, (y + e) % 4], y_in.at[a, d, 4 - e], at_y(e), YS, got_y.at[a, d])
+            put(part_b.at[a, d, (i + e) % 4], y_in.at[a, d, 4 - e], at(e), FIRST, got_y.at[a, d])
 
     def sum_over_y(a, d):
         arrive(y_in.at[a, d, pl.ds(1, 3)], got_y.at[a, d])
-        total = part_f[a, d, y]
+        first, _, i, at = axes(a, d)
+        total = part_f[a, d, first]
         for e in (1, 2, 3):
             total = total + y_in[a, d, e].astype(F32)
         for q in range(4):
@@ -171,11 +197,12 @@
             half_f[a, d, q] = rows
             half_b[a, d, q] = rows.astype(BF16)
         for e in (2, 1, 3):
-            put(half_b.at[a, d, (zl + e) % 4], z_in.at[a, d, 4 - e], at_zl(e), ZS, got_z.at[a, d])
+            put(half_b.at[a, d, (i + e) % 4], z_in.at[a, d, 4 - e], at(e), SECOND, got_z.at[a, d])
 
     def activate(a, d):
         arrive(z_in.at[a, d, pl.ds(1, 3)], got_z.at[a, d])
-        total = half_f[a, d, zl]
+        i, at_i, j, at_j = axes(a, d)
+        total = half_f[a, d, j]
         for e in (1, 2, 3):
             total = total + z_in[a, d, e].astype(F32)
         if a == 0:
@@ -186,19 +213,20 @@
             s = sigmoid_2u(v)
             slope = 1.5957691216057308 * (1.0 + 0.134145 * (v * v))
             value = (s + v * (s * (1.0 - s)) * slope) * total
-        hid[a, d, y, zl] = value.astype(BF16)
-        slot = hid.at[a, d, y, zl]
-        for e in (1, 2, 3):
-            put(slot, slot, at_zl(e), GZ, got_gz.at[a, d, e])
+        hid[a, d, i, j] = value.astype(BF16)
+        slot = hid.at[a, d, i, j]
+        for e in (1, 2, 3):
+            put(slot, slot, at_j(e), GATHER, got_gz.at[a, d, e - 1])
         for e in (1, 3, 2):
-            put(slot, slot, at_y(e), GY, got_gy.at[a, d])
+            put(slot, slot, at_i(e), SPREAD, got_gy.at[a, d])
 
     def pass_on(a, d):
-        for e in (1, 2, 3):
-            slot = hid.at[a, d, y, (zl + 4 - e) % 4]
-            arrive(slot, got_gz.at[a, d, e])
+        i, at, j, _ = axes(a, d)
+        for e in (1, 3, 2):
+            slot = hid.at[a, d, i, (j + 4 - e) % 4]
+            arrive(slot, got_gz.at[a, d, e - 1])
             for f in (1, 3, 2):
-                put(slot, slot, at_y(f), GY, got_gy.at[a, d])
+                put(slot, slot, at(f), SPREAD, got_gy.at[a, d])
 
     def second_product(a, d):
         arrive(hid.at[a, d, pl.ds(0, 3)], got_gy.at[a, d])
@@ -207,23 +235,40 @@
         value = nn(left, w_out[...]) if a == 0 else nt(left, w_in[...])
         mine[a, d] = lanes_to_rows(value[:40])
         sib_out[a, d] = lanes_to_rows(value[40:])
-        put(sib_out.at[a, d], sib_in.at[a, d], sibling, PAIR, got_pair.at[a, d])
+        if d < 3:
+            put(sib_out.at[a, d], sib_in.at[a, d], sibling, PAIR, got_pair.at[a, d])
+        else:
+            for e in (2, 1, 3, 0):
+                to_x(a, 3, e)
+                for j in range(6):
+                    rows = sib_out[a, 3, pl.ds(40 * j + 10 * e, 10), :]
+                    cross[a, e, pl.ds(10 * j, 10), :] = rows
+                cross_out[a, e] = cross[a, e].astype(BF16)
+                dst = cross_in.at[a, (4 - e) % 4]
+                put(cross_out.at[a, e], dst, at_cross(e), CROSS_OUT, got_pair.at[a, 3])
+
+    def to_x(a, d, e):
+        for j in range(6):
+            piece[a, d, e, pl.ds(10 * j, 10), :] = mine[a, d, pl.ds(40 * j + 10 * e, 10), :]
+        if e:
+            x_out[a, d, e] = piece[a, d, e].astype(BF16)
+            put(x_out.at[a, d, e], x_in.at[a, d, 4 - e], at_x(e), XR, got_xr.at[a, d])
 
     def sum_over_cores(a, d):
         arrive(sib_in.at[a, d], got_pair.at[a, d])
         mine[a, d] = mine[a, d] + sib_in[a, d]
         for e in (2, 1, 3, 0):
-            for j in range(6):
-                piece[a, d, e, pl.ds(10 * j, 10), :] = mine[a, d, pl.ds(40 * j + 10 * e, 10), :]
-            if e:
-                x_out[a, d, e] = piece[a, d, e].astype(BF16)
-                put(x_out.at[a, d, e], x_in.at[a, d, 4 - e], at_x(e), XR, got_xr.at[a, d])
+            to_x(a, d, e)
 
     def sum_over_x(a, p):
         arrive(x_in.at[a, p, pl.ds(1, 3)], got_xr.at[a, p])
         total = piece[a, p, 0]
         for e in (1, 2, 3):
             total = total + x_in[a, p, e].astype(F32)
+        if p == 3:
+            arrive(cross_in.at[a], got_pair.at[a, 3])
+            for e in range(4):
+                total = total + cross_in[a, e].astype(F32)
         e = PLACES[p]
         if e:
             zh_out[a, e] = total.astype(BF16)
@@ -232,7 +277,7 @@
             piece[a, 0, 0] = total
 
     stages = (
-        from_near, from_far, to_sibling, first_product, sum_over_y, activate, pass_on,
+        relay, from_near, from_far, to_sibling, first_product, sum_over_y, activate, pass_on,
         second_product, sum_over_cores, sum_over_x,
     )
     for stage, a, p in ORDER:
@@ -251,12 +296,14 @@
         (NEAR, gath.at[0, 0, 0]),
         (FAR, gath.at[0, 0, 0, pl.ds(0, 2)]),
         (XS, gath.at[every, every, 0, pl.ds(1, 3)]),
-        (SIB, gath.at[every, every, 0]),
-        (YS, y_in.at[every, every, pl.ds(1, 3)]),
-        (ZS, z_in.at[every, every, pl.ds(1, 3)]),
-        (GZ, z_in.at[every, every, pl.ds(1, 3)]),
-        (GY, hid.at[every, every, pl.ds(0, 3)]),
+        (SIB, gath.at[every, pl.ds(0, 3), 0]),
+        (CROSS_IN, gath.at[every, 3, 1]),
+        (FIRST, y_in.at[every, every, pl.ds(1, 3)]),
+        (SECOND, z_in.at[every, every, pl.ds(1, 3)]),
+        (GATHER, z_in.at[every, every, pl.ds(1, 3)]),
+        (SPREAD, hid.at[every, every, pl.ds(0, 3)]),
         (PAIR, sib_in),
+        (CROSS_OUT, cross_in),
         (XR, x_in.at[every, every, pl.ds(1, 3)]),
         (ZR, zh_in.at[every, pl.ds(1, 3)]),
     ):
@@ -291,22 +338,25 @@
             pltpu.VMEM((4, 32, 128), F32),
             pltpu.VMEM((2, 4, 4, 4, 32, 128), BF16),
             pltpu.VMEM((2, 4, 240, 128), F32),
-            pltpu.VMEM((2, 4, 240, 128), F32),
+            pltpu.VMEM((2, 3, 240, 128), F32),
             pltpu.VMEM((2, 4, 4, 64, 128), BF16),
             pltpu.VMEM((2, 4, 4, 64, 128), BF16),
             pltpu.VMEM((2, 4, 240, 128), F32),
             pltpu.VMEM((2, 4, 4, 64, 128), F32),
+            pltpu.VMEM((2, 4, 64, 128), F32),
+            pltpu.VMEM((2, 4, 64, 128), BF16),
+            pltpu.VMEM((2, 4, 64, 128), BF16),
             pltpu.VMEM((2, 4, 64, 128), BF16),
             pltpu.VMEM((2, 4, 64, 128), BF16),
             pltpu.SemaphoreType.DMA((6,)),
-            pltpu.SemaphoreType.DMA((11,)),
-            pltpu.SemaphoreType.DMA((2, 2)),
+            pltpu.SemaphoreType.DMA((13,)),
+            pltpu.SemaphoreType.DMA((2, 4)),
             pltpu.SemaphoreType.DMA((2,)),
             pltpu.SemaphoreType.DMA((2, 4)),
             pltpu.SemaphoreType.DMA((2, 4)),
             pltpu.SemaphoreType.DMA((2, 4)),
             pltpu.SemaphoreType.DMA((2, 4)),
-            pltpu.SemaphoreType.DMA((2, 4, 4)),
+            pltpu.SemaphoreType.DMA((2, 4, 3)),
             pltpu.SemaphoreType.DMA((2, 4)),
             pltpu.SemaphoreType.DMA((2, 4)),
             pltpu.SemaphoreType.DMA((2, 4)),

time: 65.5 us -> 64.6 us (0.986)
  Pallas kernels: 63.3 us -> 62.4 us
    pallas_call x1, Pallas kernels: 63.3 us -> 62.4 us  [on_device(): pl.pallas_call(kernel, out_shape=shape, in_specs=[hbm] * 6, out_specs=vme...]
where the time goes in v5:
time: 64.6 us; the launch traced here: 64.4 us
  Pallas kernels  62.4 us (97%)
  local copies, waits for them, and re-layouts  1.38 us (2%)
    pallas_call x1, Pallas kernels, on_device(): pl.pallas_call(kernel, out_shape=shape, in_specs=[hbm] * 6, out_specs=vme...  62.4 us
    squeeze x1, local copies, waits for them, and re-layouts, on_device(): return (o[0], o[1])  1.38 us

profile of v5, /device:TPU:1, one launch (start us, length us, event | category | flops | bytes accessed | tf_op | source)
XLA Modules:
  0.0 64.4 jit_solution(10342475869407562953)
XLA Ops:
  0.6 62.4 %shard_map.77 = bf16[2,10,768]{2,1,0:T(8,128)(2,1)} custom-call(s32[6,6]{1,0:T(8,128)} %mask_in_hbm.1, s32[6,6]{1,0:T(8,128)} %mask_out_hbm.1, bf16[10,768]{1,0:T(8,128)(2,1)} %tok_hbm.1, bf16[10,768]{1,0:T(8,128)(2,1)} %grad_hbm.1, bf16[768,768]{1,0:T(8,128)(2,1)} %w_in_hbm.1, bf16[768,768]{1,0:T(8,128)(2,1)} %w_out_hbm.1), custom_call_target="tpu_custom_call" | custom-call | tf_op jit(solution)/shard_map/pallas_call | solution.py:317
  63.0 1.4 %slice_bitcast_fusion = (bf16[10,768]{1,0:T(8,128)(2,1)}, bf16[10,768]{1,0:T(8,128)(2,1)}) fusion(bf16[2,10,768]{2,1,0:T(8,128)(2,1)} %shard_map.77), kind=kLoop, calls=%fused_computation | loop fusion | bytes 61440 | tf_op jit(solution)/shard_map/squeeze | solution.py:369

commit v6 on v5

--- a/solution.py
+++ b/solution.py
@@ -313,7 +313,7 @@
 def on_device(tokens, weight_in, weight_out, mask_in, mask_out, grad_out):
     vmem = pl.BlockSpec(memory_space=pltpu.VMEM)
     hbm = pl.BlockSpec(memory_space=pltpu.HBM)
-    shape = jax.ShapeDtypeStruct((2,) + tokens.shape, BF16)
+    shape = pltpu.VMEM((2,) + tokens.shape, BF16)
     o = pl.pallas_call(
         kernel,
         out_shape=shape,

time: 64.6 us -> 63.2 us (0.978)
  local copies, waits for them, and re-layouts: 1.38 us -> 0.62 us
    squeeze x1, local copies, waits for them, and re-layouts: 1.38 us -> 0.62 us  [on_device(): return (o[0], o[1])]
where the time goes in v6:
time: 63.2 us; the launch traced here: 63 us
  Pallas kernels  61.8 us (98%)
  between operations  0.64 us (1%)
    pallas_call x1, Pallas kernels, on_device(): pl.pallas_call(kernel, out_shape=shape, in_specs=[hbm] * 6, out_specs=vme...  61.8 us

profile of v6, /device:TPU:1, one launch (start us, length us, event | category | flops | bytes accessed | tf_op | source)
XLA Modules:
  0.0 63.0 jit_solution(8172712348983472704)
XLA Ops:
  0.6 61.8 %shard_map.77 = bf16[2,10,768]{2,1,0:T(8,128)(2,1)S(1)} custom-call(s32[6,6]{1,0:T(8,128)} %mask_in_hbm.1, s32[6,6]{1,0:T(8,128)} %mask_out_hbm.1, bf16[10,768]{1,0:T(8,128)(2,1)} %tok_hbm.1, bf16[10,768]{1,0:T(8,128)(2,1)} %grad_hbm.1, bf16[768,768]{1,0:T(8,128)(2,1)} %w_in_hbm.1, bf16[768,768]{1,0:T(8,128)(2,1)} %w_out_hbm.1), custom_call_target="tpu_custom_call" | custom-call | tf_op jit(solution)/shard_map/pallas_call | solution.py:317
  62.4 0.6 slice_bitcast_fusion

commit v7 on v6

--- a/solution.py
+++ b/solution.py
@@ -11,15 +11,17 @@
 ORDER = (
     (3, 0, 0), (0, 0, 0), (4, 0, 0), (0, 1, 0), (3, 1, 0), (1, 0, 0), (1, 1, 0), (4, 1, 0),
     (2, 0, 3), (3, 0, 1), (5, 0, 0), (3, 0, 2), (4, 0, 1), (2, 1, 3), (4, 0, 2), (5, 1, 0),
-    (3, 1, 2), (3, 1, 1), (6, 0, 0), (4, 0, 3), (4, 1, 1), (4, 1, 3), (4, 1, 2), (6, 1, 0),
-    (5, 0, 1), (5, 0, 2), (5, 0, 3), (5, 1, 3), (5, 1, 2), (5, 1, 1), (7, 1, 0), (6, 0, 2),
-    (6, 0, 3), (6, 0, 1), (6, 1, 3), (6, 1, 2), (6, 1, 1), (7, 0, 2), (7, 0, 3), (7, 0, 1),
-    (7, 1, 3), (7, 1, 1), (7, 1, 2), (7, 0, 0), (8, 1, 0), (8, 0, 2), (8, 0, 3), (9, 0, 2),
-    (8, 0, 1), (8, 1, 3), (9, 1, 0), (8, 1, 2), (8, 1, 1), (9, 0, 1), (10, 0, 3), (8, 0, 0),
-    (9, 1, 2), (9, 1, 1), (10, 0, 2), (10, 1, 3), (10, 0, 1), (9, 0, 0), (10, 1, 2), (10, 1, 0),
-    (10, 1, 1), (10, 0, 0),
+    (3, 1, 2), (3, 1, 1), (6, 0, 0), (4, 0, 3), (4, 0, 4), (4, 1, 1), (4, 1, 3), (4, 1, 4),
+    (4, 1, 2), (6, 1, 0), (5, 0, 1), (5, 0, 2), (5, 0, 3), (5, 0, 4), (5, 1, 3), (5, 1, 4),
+    (5, 1, 2), (5, 1, 1), (6, 0, 2), (6, 0, 3), (6, 0, 4), (6, 0, 1), (6, 1, 3), (7, 1, 0),
+    (6, 1, 4), (6, 1, 2), (6, 1, 1), (7, 0, 2), (7, 0, 3), (7, 0, 4), (7, 0, 1), (7, 1, 3),
+    (7, 1, 4), (7, 1, 1), (7, 1, 2), (7, 0, 0), (8, 1, 0), (8, 0, 2), (8, 0, 3), (8, 0, 4),
+    (9, 0, 2), (8, 0, 1), (8, 1, 3), (8, 1, 4), (9, 1, 0), (8, 1, 2), (8, 1, 1), (9, 0, 1),
+    (10, 0, 3), (8, 0, 0), (9, 1, 2), (9, 1, 1), (10, 0, 2), (10, 1, 3), (10, 0, 1), (9, 0, 0),
+    (10, 1, 2), (10, 1, 0), (10, 1, 1), (10, 0, 0),
 )
-NEAR, FAR, XS, SIB, FIRST, SECOND, GATHER, SPREAD, PAIR, XR, ZR, CROSS_IN, CROSS_OUT = range(13)
+NEAR, FAR, XS, SIB, PAIR, XR, ZR, CROSS_IN, CROSS_OUT = range(9)
+FIRST, SECOND, GATHER, SPREAD = 9, 11, 13, 15
 Z_FIRST = ((0, 1), (1, 1))
 
 
@@ -45,9 +47,9 @@
 def kernel(
     mask_in_hbm, mask_out_hbm, tok_hbm, grad_hbm, w_in_hbm, w_out_hbm, out,
     mask_in, mask_out, tok, grad, w_in, w_out, gath, pack, unp, part_f, part_b, y_in,
-    half_f, half_b, z_in, pre_s, hid, sib_out, sib_in, x_out, x_in, mine, piece, cross,
+    half_f, half_b, z_in, hid, far_part_f, far_part_b, far_y_in, far_half_f, far_half_b, far_z_in, far_hid, pre_s, sib_out, sib_in, x_out, x_in, mine, piece, cross,
     cross_out, cross_in, zh_out, zh_in,
-    load_sem, send, got_near, got_far, got_x, got_sib, got_y, got_z, got_gz, got_gy, got_pair, got_xr,
+    send, got_near, got_far, got_x, got_sib, got_y, got_z, got_gz, got_far_gz, got_pair, got_xr,
     got_zr,
 ):
     r, c = lax.axis_index("row"), lax.axis_index("col")
@@ -93,7 +95,7 @@
         (w_in_hbm, w_in),
         (w_out_hbm, w_out),
     ):
-        loads.append(pltpu.make_async_copy(src, dst, load_sem.at[len(loads)]))
+        loads.append(pltpu.make_async_copy(src, dst, send.at[FIRST + len(loads)]))
         loads[-1].start()
 
     def put(src, dst, peer, kind, sem):
@@ -121,25 +123,22 @@
     def spread(a, p):
         for e in (2, 1, 3):
             put(gath.at[a, p, 0, 0], gath.at[a, p, 0, 4 - e], at_x(e), XS, got_x.at[a, p])
-            if p == 3:
-                dst = gath.at[a, 3, 1, 4 - e]
+        if p == 3:
+            for e in (2, 1, 3, 0):
+                dst = gath.at[a, 3, 1, (4 - e) % 4]
                 put(gath.at[a, 3, 0, 0], dst, at_cross(e), CROSS_IN, got_sib.at[a, 3])
-        if p == 3:
-            put(gath.at[a, 3, 0, 0], gath.at[a, 3, 1, 0], sibling, CROSS_IN, got_sib.at[a, 3])
 
     top, low = pl.ds(0, 32), pl.ds(32, 32)
 
     def relay(a, _):
         far = gath.at[a, 3, 0, 0]
-        arrive(gath.at[a, 1, 0, 0, top], got_near.at[a, 0])
+        arrive(gath.at[a, 1, 0, 0], got_near.at[a, 0])
         put(gath.at[a, 1, 0, 0, top], far.at[top], at_zh(3), FAR, got_far.at[a])
-        arrive(gath.at[a, 2, 0, 0, low], got_near.at[a, 1])
         put(gath.at[a, 2, 0, 0, low], far.at[low], at_zh(1), FAR, got_far.at[a])
 
     def from_near(a, _):
-        arrive(gath.at[a, 1, 0, 0, low], got_near.at[a, 2])
+        arrive(gath.at[a, 1, 0, 0], got_near.at[a, 1])
         spread(a, 1)
-        arrive(gath.at[a, 2, 0, 0, top], got_near.at[a, 3])
         spread(a, 2)
 
     def from_far(a, p):
@@ -150,11 +149,11 @@
         arrive(gath.at[a, p, 0, pl.ds(1, 3)], got_x.at[a, p])
         put(gath.at[a, p, 0], gath.at[a, p, 1], sibling, SIB, got_sib.at[a, p])
 
-    for i, halves in ((0, (top, low)), (2, (low, top))):
+    for i, halves in enumerate(((top, low), (low, top))):
         for a in (0, 1):
             own = gath.at[a, 0, 0, 0]
-            for j, p, half, e in ((i, 1, halves[0], 3), (i + 1, 2, halves[1], 1)):
-                put(own.at[half], gath.at[a, p, 0, 0, half], at_zh(e), NEAR, got_near.at[a, j])
+            for p, half, e in ((1, halves[0], 3), (2, halves[1], 1)):
+                put(own.at[half], gath.at[a, p, 0, 0, half], at_zh(e), NEAR, got_near.at[a, i])
     for a in (0, 1):
         spread(a, 0)
     for load in loads[2:]:
@@ -167,79 +166,115 @@
                 keep = mask[i, j].astype(F32)
                 w[rows, cols] = (w[rows, cols].astype(F32) * keep).astype(BF16)
 
-    def first_product(a, d):
-        if d == 3:
+    near_bank = (part_f, part_b, y_in, half_f, half_b, z_in, hid)
+    far_bank = (far_part_f, far_part_b, far_y_in, far_half_f, far_half_b, far_z_in, far_hid)
+
+    def bank(p):
+        return (near_bank, p, 80, 128, 0) if p < 3 else (far_bank, p - 3, 40, 64, 1)
+
+    def first_product(a, p):
+        (f, b, y_in, *_), u, n, wide, kind = bank(p)
+        if p == 3:
             arrive(gath.at[a, 3, 0, pl.ds(1, 3)], got_x.at[a, 3])
-        arrive(gath.at[a, d, 1], got_sib.at[a, d])
-        for s in range(8):
-            unp[a, pl.ds(60 * s, 60), :] = gath[a, d, s // 4, s % 4].astype(F32)[:60]
+            slots = [(3, 0, s) for s in range(4)]
+        elif p == 4:
+            arrive(gath.at[a, 3, 1], got_sib.at[a, 3])
+            slots = [(3, 1, s) for s in range(4)]
+        else:
+            arrive(gath.at[a, p, 1], got_sib.at[a, p])
+            slots = [(p, s // 4, s % 4) for s in range(8)]
+        for s, slot in enumerate(slots):
+            unp[a, pl.ds(60 * s, 60), :] = gath[(a, *slot)].astype(F32)[:60]
         left = jnp.concatenate(
-            [unp[a, pl.ds(j, 80, stride=6), :].astype(BF16) for j in range(6)], axis=1
-        ).astype(BF16)
+            [unp[a, pl.ds(j, n, stride=6), :].astype(BF16) for j in range(6)], axis=1
+        )
         value = nn(left, w_in[...]) if a == 0 else nt(left, w_out[...])
-        rows = jnp.concatenate([lanes_to_rows(value), jnp.zeros((32, 128), F32)], axis=0)
+        fill = jnp.zeros((4 * wide - 6 * n, 128), F32)
+        rows = jnp.concatenate([lanes_to_rows(value), fill], axis=0)
         for g in range(4):
-            part = rows[128 * g : 128 * (g + 1)]
-            part_f[a, d, g] = part
-            part_b[a, d, g] = part.astype(BF16)
-        i, at, _, _ = axes(a, d)
+            part = rows[wide * g : wide * (g + 1)]
+            f[a, u, g] = part
+            b[a, u, g] = part.astype(BF16)
+        i, at, _, _ = axes(a, p)
         for e in (2, 1, 3):
-            put(part_b.at[a, d, (i + e) % 4], y_in.at[a, d, 4 - e], at(e), FIRST, got_y.at[a, d])
-
-    def sum_over_y(a, d):
-        arrive(y_in.at[a, d, pl.ds(1, 3)], got_y.at[a, d])
-        first, _, i, at = axes(a, d)
-        total = part_f[a, d, first]
+            put(b.at[a, u, (i + e) % 4], y_in.at[a, u, 4 - e], at(e), FIRST + kind, got_y.at[a, p])
+
+    def sum_over_y(a, p):
+        (f, _, y_in, half_f, half_b, z_in, _), u, _, wide, kind = bank(p)
+        arrive(y_in.at[a, u, pl.ds(1, 3)], got_y.at[a, p])
+        first, _, i, at = axes(a, p)
+        total = f[a, u, first]
         for e in (1, 2, 3):
-            total = total + y_in[a, d, e].astype(F32)
+            total = total + y_in[a, u, e].astype(F32)
         for q in range(4):
-            rows = total[32 * q : 32 * (q + 1)]
-            half_f[a, d, q] = rows
-            half_b[a, d, q] = rows.astype(BF16)
+            rows = total[wide // 4 * q : wide // 4 * (q + 1)]
+            half_f[a, u, q] = rows
+            half_b[a, u, q] = rows.astype(BF16)
         for e in (2, 1, 3):
-            put(half_b.at[a, d, (i + e) % 4], z_in.at[a, d, 4 - e], at(e), SECOND, got_z.at[a, d])
-
-    def activate(a, d):
-        arrive(z_in.at[a, d, pl.ds(1, 3)], got_z.at[a, d])
-        i, at_i, j, at_j = axes(a, d)
-        total = half_f[a, d, j]
+            src, dst = half_b.at[a, u, (i + e) % 4], z_in.at[a, u, 4 - e]
+            put(src, dst, at(e), SECOND + kind, got_z.at[a, p])
+
+    def gathered(a, p, e):
+        if e == 1:
+            return got_y.at[a, p]
+        if e == 2:
+            return got_sib.at[a, p] if p < 3 else got_far_gz.at[a, p - 3]
+        return got_gz.at[a, p]
+
+    def spreads(a, p):
+        return got_x.at[a, p] if p < 4 else got_sib.at[a, 3]
+
+    def activate(a, p):
+        (_, _, _, half_f, _, z_in, hid), u, _, wide, kind = bank(p)
+        arrive(z_in.at[a, u, pl.ds(1, 3)], got_z.at[a, p])
+        i, at_i, j, at_j = axes(a, p)
+        total = half_f[a, u, j]
         for e in (1, 2, 3):
-            total = total + z_in[a, d, e].astype(F32)
+            total = total + z_in[a, u, e].astype(F32)
         if a == 0:
-            pre_s[d] = total
+            pre_s[p, pl.ds(0, wide // 4), :] = total
             value = total * sigmoid_2u(total)
         else:
-            v = pre_s[d]
+            v = pre_s[p, pl.ds(0, wide // 4), :]
             s = sigmoid_2u(v)
             slope = 1.5957691216057308 * (1.0 + 0.134145 * (v * v))
             value = (s + v * (s * (1.0 - s)) * slope) * total
-        hid[a, d, i, j] = value.astype(BF16)
-        slot = hid.at[a, d, i, j]
+        hid[a, u, i, j] = value.astype(BF16)
+        slot = hid.at[a, u, i, j]
         for e in (1, 2, 3):
-            put(slot, slot, at_j(e), GATHER, got_gz.at[a, d, e - 1])
+            put(slot, slot, at_j(e), GATHER + kind, gathered(a, p, e))
         for e in (1, 3, 2):
-            put(slot, slot, at_i(e), SPREAD, got_gy.at[a, d])
-
-    def pass_on(a, d):
-        i, at, j, _ = axes(a, d)
+            put(slot, slot, at_i(e), SPREAD + kind, spreads(a, p))
+
+    def pass_on(a, p):
+        (*_, hid), u, _, _, kind = bank(p)
+        i, at, j, _ = axes(a, p)
         for e in (1, 3, 2):
-            slot = hid.at[a, d, i, (j + 4 - e) % 4]
-            arrive(slot, got_gz.at[a, d, e - 1])
+            slot = hid.at[a, u, i, (j + 4 - e) % 4]
+            arrive(slot, gathered(a, p, e))
             for f in (1, 3, 2):
-                put(slot, slot, at(f), SPREAD, got_gy.at[a, d])
-
-    def second_product(a, d):
-        arrive(hid.at[a, d, pl.ds(0, 3)], got_gy.at[a, d])
-        rows = hid[a, d].reshape(512, 128)
-        left = jnp.concatenate([rows[80 * j : 80 * (j + 1)] for j in range(6)], axis=1)
+                put(slot, slot, at(f), SPREAD + kind, spreads(a, p))
+
+    def second_product(a, p):
+        (*_, hid), u, n, wide, _ = bank(p)
+        arrive(hid.at[a, u, pl.ds(0, 3)], spreads(a, p))
+        rows = hid[a, u].reshape(4 * wide, 128)
+        if n % 16:
+            rows = rows.astype(F32)
+        left = jnp.concatenate([rows[n * j : n * (j + 1)] for j in range(6)], axis=1)
+        left = left.astype(BF16)
         value = nn(left, w_out[...]) if a == 0 else nt(left, w_in[...])
-        mine[a, d] = lanes_to_rows(value[:40])
-        sib_out[a, d] = lanes_to_rows(value[40:])
-        if d < 3:
-            put(sib_out.at[a, d], sib_in.at[a, d], sibling, PAIR, got_pair.at[a, d])
-        else:
+        if p < 3:
+            mine[a, p] = lanes_to_rows(value[:40])
+            sib_out[a, p] = lanes_to_rows(value[40:])
+            put(sib_out.at[a, p], sib_in.at[a, p], sibling, PAIR, got_pair.at[a, p])
+        elif p == 3:
+            mine[a, 3] = lanes_to_rows(value)
             for e in (2, 1, 3, 0):
                 to_x(a, 3, e)
+        else:
+            sib_out[a, 3] = lanes_to_rows(value)
+            for e in (2, 1, 3, 0):
                 for j in range(6):
                     rows = sib_out[a, 3, pl.ds(40 * j + 10 * e, 10), :]
                     cross[a, e, pl.ds(10 * j, 10), :] = rows
@@ -299,9 +334,13 @@
         (SIB, gath.at[every, pl.ds(0, 3), 0]),
         (CROSS_IN, gath.at[every, 3, 1]),
         (FIRST, y_in.at[every, every, pl.ds(1, 3)]),
+        (FIRST + 1, far_y_in.at[every, every, pl.ds(1, 3)]),
         (SECOND, z_in.at[every, every, pl.ds(1, 3)]),
+        (SECOND + 1, far_z_in.at[every, every, pl.ds(1, 3)]),
         (GATHER, z_in.at[every, every, pl.ds(1, 3)]),
+        (GATHER + 1, far_z_in.at[every, every, pl.ds(1, 3)]),
         (SPREAD, hid.at[every, every, pl.ds(0, 3)]),
+        (SPREAD + 1, far_hid.at[every, every, pl.ds(0, 3)]),
         (PAIR, sib_in),
         (CROSS_OUT, cross_in),
         (XR, x_in.at[every, every, pl.ds(1, 3)]),
@@ -329,14 +368,21 @@
             pltpu.VMEM((2, 4, 2, 4, 64, 128), BF16),
             pltpu.VMEM((2, 64, 128), F32),
             pltpu.VMEM((2, 480, 128), F32),
-            pltpu.VMEM((2, 4, 4, 128, 128), F32),
-            pltpu.VMEM((2, 4, 4, 128, 128), BF16),
-            pltpu.VMEM((2, 4, 4, 128, 128), BF16),
-            pltpu.VMEM((2, 4, 4, 32, 128), F32),
-            pltpu.VMEM((2, 4, 4, 32, 128), BF16),
-            pltpu.VMEM((2, 4, 4, 32, 128), BF16),
-            pltpu.VMEM((4, 32, 128), F32),
-            pltpu.VMEM((2, 4, 4, 4, 32, 128), BF16),
+            pltpu.VMEM((2, 3, 4, 128, 128), F32),
+            pltpu.VMEM((2, 3, 4, 128, 128), BF16),
+            pltpu.VMEM((2, 3, 4, 128, 128), BF16),
+            pltpu.VMEM((2, 3, 4, 32, 128), F32),
+            pltpu.VMEM((2, 3, 4, 32, 128), BF16),
+            pltpu.VMEM((2, 3, 4, 32, 128), BF16),
+            pltpu.VMEM((2, 3, 4, 4, 32, 128), BF16),
+            pltpu.VMEM((2, 2, 4, 64, 128), F32),
+            pltpu.VMEM((2, 2, 4, 64, 128), BF16),
+            pltpu.VMEM((2, 2, 4, 64, 128), BF16),
+            pltpu.VMEM((2, 2, 4, 16, 128), F32),
+            pltpu.VMEM((2, 2, 4, 16, 128), BF16),
+            pltpu.VMEM((2, 2, 4, 16, 128), BF16),
+            pltpu.VMEM((2, 2, 4, 4, 16, 128), BF16),
+            pltpu.VMEM((5, 32, 128), F32),
             pltpu.VMEM((2, 4, 240, 128), F32),
             pltpu.VMEM((2, 3, 240, 128), F32),
             pltpu.VMEM((2, 4, 4, 64, 128), BF16),
@@ -348,16 +394,15 @@
             pltpu.VMEM((2, 4, 64, 128), BF16),
             pltpu.VMEM((2, 4, 64, 128), BF16),
             pltpu.VMEM((2, 4, 64, 128), BF16),
-            pltpu.SemaphoreType.DMA((6,)),
-            pltpu.SemaphoreType.DMA((13,)),
-            pltpu.SemaphoreType.DMA((2, 4)),
+            pltpu.SemaphoreType.DMA((17,)),
+            pltpu.SemaphoreType.DMA((2, 2)),
             pltpu.SemaphoreType.DMA((2,)),
             pltpu.SemaphoreType.DMA((2, 4)),
             pltpu.SemaphoreType.DMA((2, 4)),
-            pltpu.SemaphoreType.DMA((2, 4)),
-            pltpu.SemaphoreType.DMA((2, 4)),
-            pltpu.SemaphoreType.DMA((2, 4, 3)),
-            pltpu.SemaphoreType.DMA((2, 4)),
+            pltpu.SemaphoreType.DMA((2, 5)),
+            pltpu.SemaphoreType.DMA((2, 5)),
+            pltpu.SemaphoreType.DMA((2, 5)),
+            pltpu.SemaphoreType.DMA((2, 2)),
             pltpu.SemaphoreType.DMA((2, 4)),
             pltpu.SemaphoreType.DMA((2, 4)),
             pltpu.SemaphoreType.DMA((2,)),

time: 63.2 us -> 61.4 us (0.972)
  Pallas kernels: 61.8 us -> 59.7 us
    pallas_call x1, Pallas kernels: 61.8 us -> 59.7 us  [on_device(): pl.pallas_call(kernel, out_shape=shape, in_specs=[hbm] * 6, out_specs=vme...]
where the time goes in v7:
time: 61.4 us; the launch traced here: 61 us
  Pallas kernels  59.7 us (97%)
  between operations  0.64 us (1%)
  local copies, waits for them, and re-layouts  0.62 us (1%)
    pallas_call x1, Pallas kernels, on_device(): pl.pallas_call(kernel, out_shape=shape, in_specs=[hbm] * 6, out_specs=vme...  59.7 us

profile of v7, /device:TPU:1, one launch (start us, length us, event | category | flops | bytes accessed | tf_op | source)
XLA Modules:
  0.0 61.0 jit_solution(6991664790938038288)
XLA Ops:
  0.6 59.7 %shard_map.77 = bf16[2,10,768]{2,1,0:T(8,128)(2,1)S(1)} custom-call(s32[6,6]{1,0:T(8,128)} %mask_in_hbm.1, s32[6,6]{1,0:T(8,128)} %mask_out_hbm.1, bf16[10,768]{1,0:T(8,128)(2,1)} %tok_hbm.1, bf16[10,768]{1,0:T(8,128)(2,1)} %grad_hbm.1, bf16[768,768]{1,0:T(8,128)(2,1)} %w_in_hbm.1, bf16[768,768]{1,0:T(8,128)(2,1)} %w_out_hbm.1), custom_call_target="tpu_custom_call" | custom-call | tf_op jit(solution)/shard_map/pallas_call | solution.py:356
  60.4 0.6 %slice_bitcast_fusion = (bf16[10,768]{1,0:T(8,128)(2,1)}, bf16[10,768]{1,0:T(8,128)(2,1)}) fusion(bf16[2,10,768]{2,1,0:T(8,128)(2,1)S(1)} %shard_map.77), kind=kLoop, calls=%fused_computation | loop fusion | bytes 61440 | tf_op jit(solution)/shard_map/squeeze | solution.py:414

commit v8 on v7

--- a/solution.py
+++ b/solution.py
@@ -366,8 +366,8 @@
             pltpu.VMEM((768, 768), BF16),
             pltpu.VMEM((768, 768), BF16),
             pltpu.VMEM((2, 4, 2, 4, 64, 128), BF16),
-            pltpu.VMEM((2, 64, 128), F32),
-            pltpu.VMEM((2, 480, 128), F32),
+            pltpu.VMEM((4, 64, 128), F32),
+            pltpu.VMEM((3, 480, 128), F32),
             pltpu.VMEM((2, 3, 4, 128, 128), F32),
             pltpu.VMEM((2, 3, 4, 128, 128), BF16),
             pltpu.VMEM((2, 3, 4, 128, 128), BF16),
@@ -383,13 +383,13 @@
             pltpu.VMEM((2, 2, 4, 16, 128), BF16),
             pltpu.VMEM((2, 2, 4, 4, 16, 128), BF16),
             pltpu.VMEM((5, 32, 128), F32),
-            pltpu.VMEM((2, 4, 240, 128), F32),
+            pltpu.VMEM((3, 4, 240, 128), F32),
             pltpu.VMEM((2, 3, 240, 128), F32),
             pltpu.VMEM((2, 4, 4, 64, 128), BF16),
             pltpu.VMEM((2, 4, 4, 64, 128), BF16),
-            pltpu.VMEM((2, 4, 240, 128), F32),
-            pltpu.VMEM((2, 4, 4, 64, 128), F32),
-            pltpu.VMEM((2, 4, 64, 128), F32),
+            pltpu.VMEM((3, 4, 240, 128), F32),
+            pltpu.VMEM((3, 4, 4, 64, 128), F32),
+            pltpu.VMEM((3, 4, 64, 128), F32),
             pltpu.VMEM((2, 4, 64, 128), BF16),
             pltpu.VMEM((2, 4, 64, 128), BF16),
             pltpu.VMEM((2, 4, 64, 128), BF16),

time: 61.4 us -> 61.4 us (level)
  no operation moved by 1% of the time
where the time goes in v8:
time: 61.4 us; the launch traced here: 61 us
  Pallas kernels  59.7 us (97%)
  between operations  0.64 us (1%)
  local copies, waits for them, and re-layouts  0.62 us (1%)
    pallas_call x1, Pallas kernels, on_device(): pl.pallas_call(kernel, out_shape=shape, in_specs=[hbm] * 6, out_specs=vme...  59.7 us

profile of v8, /device:TPU:1, one launch (start us, length us, event | category | flops | bytes accessed | tf_op | source)
XLA Modules:
  0.0 61.0 jit_solution(8661643978744596569)
XLA Ops:
  0.6 59.7 %shard_map.77 = bf16[2,10,768]{2,1,0:T(8,128)(2,1)S(1)} custom-call(s32[6,6]{1,0:T(8,128)} %mask_in_hbm.1, s32[6,6]{1,0:T(8,128)} %mask_out_hbm.1, bf16[10,768]{1,0:T(8,128)(2,1)} %tok_hbm.1, bf16[10,768]{1,0:T(8,128)(2,1)} %grad_hbm.1, bf16[768,768]{1,0:T(8,128)(2,1)} %w_in_hbm.1, bf16[768,768]{1,0:T(8,128)(2,1)} %w_out_hbm.1), custom_call_target="tpu_custom_call" | custom-call | tf_op jit(solution)/shard_map/pallas_call | solution.py:356
  60.4 0.6 %slice_bitcast_fusion = (bf16[10,768]{1,0:T(8,128)(2,1)}, bf16[10,768]{1,0:T(8,128)(2,1)}) fusion(bf16[2,10,768]{2,1,0:T(8,128)(2,1)S(1)} %shard_map.77), kind=kLoop, calls=%fused_computation | loop fusion | bytes 61440 | tf_op jit(solution)/shard_map/squeeze | solution.py:414

commit v9 on v8

--- a/solution.py
+++ b/solution.py
@@ -12,7 +12,7 @@
     (3, 0, 0), (0, 0, 0), (4, 0, 0), (0, 1, 0), (3, 1, 0), (1, 0, 0), (1, 1, 0), (4, 1, 0),
     (2, 0, 3), (3, 0, 1), (5, 0, 0), (3, 0, 2), (4, 0, 1), (2, 1, 3), (4, 0, 2), (5, 1, 0),
     (3, 1, 2), (3, 1, 1), (6, 0, 0), (4, 0, 3), (4, 0, 4), (4, 1, 1), (4, 1, 3), (4, 1, 4),
-    (4, 1, 2), (6, 1, 0), (5, 0, 1), (5, 0, 2), (5, 0, 3), (5, 0, 4), (5, 1, 3), (5, 1, 4),
+    (4, 1, 2), (5, 0, 1), (5, 0, 2), (5, 0, 3), (5, 0, 4), (6, 1, 0), (5, 1, 3), (5, 1, 4),
     (5, 1, 2), (5, 1, 1), (6, 0, 2), (6, 0, 3), (6, 0, 4), (6, 0, 1), (6, 1, 3), (7, 1, 0),
     (6, 1, 4), (6, 1, 2), (6, 1, 1), (7, 0, 2), (7, 0, 3), (7, 0, 4), (7, 0, 1), (7, 1, 3),
     (7, 1, 4), (7, 1, 1), (7, 1, 2), (7, 0, 0), (8, 1, 0), (8, 0, 2), (8, 0, 3), (8, 0, 4),

time: 61.4 us -> 61.2 us (level)
  no operation moved by 1% of the time
where the time goes in v9:
time: 61.2 us; the launch traced here: 61 us
  Pallas kernels  59.8 us (98%)
  between operations  0.64 us (1%)
  local copies, waits for them, and re-layouts  0.62 us (1%)
    pallas_call x1, Pallas kernels, on_device(): pl.pallas_call(kernel, out_shape=shape, in_specs=[hbm] * 6, out_specs=vme...  59.8 us

profile of v9, /device:TPU:1, one launch (start us, length us, event | category | flops | bytes accessed | tf_op | source)
XLA Modules:
  0.0 61.0 jit_solution(13185459491760088620)
XLA Ops:
  0.6 59.8 %shard_map.77 = bf16[2,10,768]{2,1,0:T(8,128)(2,1)S(1)} custom-call(s32[6,6]{1,0:T(8,128)} %mask_in_hbm.1, s32[6,6]{1,0:T(8,128)} %mask_out_hbm.1, bf16[10,768]{1,0:T(8,128)(2,1)} %tok_hbm.1, bf16[10,768]{1,0:T(8,128)(2,1)} %grad_hbm.1, bf16[768,768]{1,0:T(8,128)(2,1)} %w_in_hbm.1, bf16[768,768]{1,0:T(8,128)(2,1)} %w_out_hbm.1), custom_call_target="tpu_custom_call" | custom-call | tf_op jit(solution)/shard_map/pallas_call | solution.py:356
  60.4 0.6 %slice_bitcast_fusion = (bf16[10,768]{1,0:T(8,128)(2,1)}, bf16[10,768]{1,0:T(8,128)(2,1)}) fusion(bf16[2,10,768]{2,1,0:T(8,128)(2,1)S(1)} %shard_map.77), kind=kLoop, calls=%fused_computation | loop fusion | bytes 61440 | tf_op jit(solution)/shard_map/squeeze | solution.py:414
